TPU v7x, 32 devices: a whole 2x2x4 slice. The times are simulated.
32 devices in a mesh: dp: 16 (over z, y, core), tensor: 2 (over x).
Axes of the slice: x: 2, y: 2, z: 4, core: 2. Of those that a mesh axis runs over, the one named last changes fastest.
Arguments:
- hidden_in: bfloat16 [24576, 768], P(('dp', 'tensor')), may hold values from -6 to 6
- seq_lens: int32 [16], P('dp'), may hold values from 864 to 1536, as said below
- ln1_gain: float32 [768], replicated, may hold values from 0.5 to 1.5
- ln1_bias: float32 [768], replicated, may hold values from -4 to 4
- w_qkv: bfloat16 [3, 768, 768], P(None, 'dp', 'tensor'), may hold values from -0.21875 to 0.21875
- bias_qv: float32 [2, 768], replicated, may hold values from -4 to 4
- w_out: bfloat16 [768, 768], P('tensor', 'dp'), may hold values from -2 to 2
- bias_out: float32 [768], replicated, may hold values from -4 to 4
- ln2_gain: float32 [768], replicated, may hold values from 0.5 to 1.5
- ln2_bias: float32 [768], replicated, may hold values from -4 to 4
- w_up: bfloat16 [768, 3072], P('dp', 'tensor'), may hold values from -0.21875 to 0.21875
- bias_up: float32 [3072], replicated, may hold values from -4 to 4
- w_down: bfloat16 [3072, 768], P('tensor', 'dp'), may hold values from -0.109375 to 0.109375
- bias_down: float32 [768], replicated, may hold values from -4 to 4
- grad_out: bfloat16 [24576, 768], P(('dp', 'tensor')), may hold values from -6 to 6
Outputs:
- out: bfloat16 [24576, 768], P(('dp', 'tensor'))
- grad_in: float32 [24576, 768], P(('dp', 'tensor'))
- grad_ln1_gain: float32 [768], replicated
- grad_ln1_bias: float32 [768], replicated
- grad_w_qkv: float32 [3, 768, 768], P(None, 'dp', 'tensor')
- grad_bias_qv: float32 [2, 768], replicated
- grad_w_out: float32 [768, 768], P('tensor', 'dp')
- grad_bias_out: float32 [768], replicated
- grad_ln2_gain: float32 [768], replicated
- grad_ln2_bias: float32 [768], replicated
- grad_w_up: float32 [768, 3072], P('dp', 'tensor')
- grad_bias_up: float32 [3072], replicated
- grad_w_down: float32 [3072, 768], P('tensor', 'dp')
- grad_bias_down: float32 [768], replicated
Inputs may be any that keep to these rules, and one draw needn't show every extreme that they name: Each index of dp holds one sequence in its first seq_lens slots, the rest being padding; some index holds exactly 1536 tokens in every draw.
All inputs are finite; a program needn't handle non-finite values.
Results may differ from a plain program's by a relative error of at most 0.02.
Values may be sent and summed in bfloat16 or wider, within the bound.
No kernel may reach another device: no remote copies, remote signals or barrier semaphores. Data moves between devices by JAX's collectives and lax.ppermute only.
A program may use at most 192 MiB of HBM per device.

v0:
```python
import math

import jax
import jax.numpy as jnp
from jax import lax
from jax.sharding import PartitionSpec as P

HD = 64
FF = 3072


epsilon = 1e-05


def layer_norm(values, gain, shift):
    center = values - jnp.mean(values, axis=-1, keepdims=True)
    spread = jnp.mean(center * center, axis=-1, keepdims=True)
    return center * lax.rsqrt(spread + epsilon) * gain + shift


def shards(
    hidden_in,
    seq_lens,
    ln1_gain,
    ln1_bias,
    w_qkv,
    bias_qv,
    w_out,
    bias_out,
    ln2_gain,
    ln2_bias,
    w_up,
    bias_up,
    w_down,
    bias_down,
    grad_out,
):
    tensor_index = lax.axis_index("tensor")
    local_rows = hidden_in.shape[0]
    width = hidden_in.shape[1]
    all_rows = local_rows * lax.axis_size("tensor")
    head_cols = w_qkv.shape[2]
    heads_here = head_cols // HD
    hidden_cols = w_up.shape[1]
    block_rows = min(512, all_rows)
    block_count = all_rows // block_rows
    score_scale = 1.0 / math.sqrt(HD)
    length = seq_lens[0]
    slot_local = tensor_index * local_rows + jnp.arange(local_rows, dtype=jnp.int32)
    valid_local = (slot_local < length).astype(jnp.float32)[:, None]
    residual_in = hidden_in.astype(jnp.float32)
    gathered = (
        lax.all_gather(w_qkv, "dp", axis=1, tiled=True),
        lax.all_gather(w_out, "dp", axis=1, tiled=True),
        lax.all_gather(w_up, "dp", axis=0, tiled=True),
        lax.all_gather(w_down, "dp", axis=1, tiled=True),
    )
    qkv_full, out_full, up_full, down_full = gathered
    normed_one = layer_norm(residual_in, ln1_gain, ln1_bias)
    normed_all = lax.all_gather(normed_one.astype(jnp.bfloat16), "tensor", axis=0, tiled=True)
    bias_local = lax.dynamic_slice_in_dim(bias_qv, tensor_index * head_cols, head_cols, 1)
    qkv_bias = jnp.stack([bias_local[0], jnp.zeros_like(bias_local[0]), bias_local[1]])
    projected = jnp.einsum("rd,cde->cre", normed_all, qkv_full, preferred_element_type=jnp.float32)
    projected = (projected + qkv_bias[:, None, :]).astype(jnp.bfloat16)
    queries = projected[0].reshape(all_rows, heads_here, HD)
    keys_all = projected[1].reshape(all_rows, heads_here, HD)
    values_all = projected[2].reshape(all_rows, heads_here, HD)
    key_slots = jnp.arange(all_rows, dtype=jnp.int32)

    def block_scores(begin_row):
        query_block = lax.dynamic_slice_in_dim(queries, begin_row, block_rows, 0)
        scores = (
            jnp.einsum("qhd,khd->hqk", query_block, keys_all, preferred_element_type=jnp.float32)
            * score_scale
        )
        query_slots = begin_row + jnp.arange(block_rows, dtype=jnp.int32)
        allowed = (key_slots[None, :] <= query_slots[:, None]) & (key_slots[None, :] < length)
        return (query_block, jnp.where(allowed[None], scores, -1000000000.0))

    def attend_forward(begin_row):
        query_block, scores = block_scores(begin_row)
        top_score = jnp.max(scores, axis=-1, keepdims=True)
        exp_scores = jnp.exp(scores - top_score)
        row_total = jnp.sum(exp_scores, axis=-1, keepdims=True)
        weights_low = (exp_scores / row_total).astype(jnp.bfloat16)
        mixed_block = jnp.einsum(
            "hqk,khd->qhd", weights_low, values_all, preferred_element_type=jnp.float32
        )
        log_total = (top_score + jnp.log(row_total))[..., 0]
        return (mixed_block.reshape(block_rows, head_cols).astype(jnp.bfloat16), log_total)

    block_starts = jnp.arange(block_count, dtype=jnp.int32) * block_rows
    mixed_blocks, log_totals = lax.map(attend_forward, block_starts)
    mixed = mixed_blocks.reshape(all_rows, head_cols)
    attn_terms = jnp.dot(mixed, out_full, preferred_element_type=jnp.float32)
    attn_local = lax.psum_scatter(
        attn_terms.astype(jnp.bfloat16), "tensor", scatter_dimension=0, tiled=True
    ).astype(jnp.float32)
    hidden_one = residual_in + attn_local + bias_out
    normed_two = layer_norm(hidden_one, ln2_gain, ln2_bias)
    normed_all_two = lax.all_gather(normed_two.astype(jnp.bfloat16), "tensor", axis=0, tiled=True)
    bias_up_local = lax.dynamic_slice_in_dim(bias_up, tensor_index * hidden_cols, hidden_cols, 0)
    pre_act = jnp.dot(normed_all_two, up_full, preferred_element_type=jnp.float32) + bias_up_local
    activated = jax.nn.gelu(pre_act).astype(jnp.bfloat16)
    mlp_terms = jnp.dot(activated, down_full, preferred_element_type=jnp.float32)
    mlp_local = lax.psum_scatter(
        mlp_terms.astype(jnp.bfloat16), "tensor", scatter_dimension=0, tiled=True
    ).astype(jnp.float32)
    layer_out = (hidden_one + mlp_local + bias_down).astype(jnp.bfloat16)
    qkv_back, out_back, up_back, down_back = (
        lax.all_gather(w_qkv, "dp", axis=1, tiled=True),
        lax.all_gather(w_out, "dp", axis=1, tiled=True),
        lax.all_gather(w_up, "dp", axis=0, tiled=True),
        lax.all_gather(w_down, "dp", axis=1, tiled=True),
    )
    grad_top = grad_out.astype(jnp.float32) * valid_local
    grad_mlp_low = grad_top.astype(jnp.bfloat16)
    grad_mlp_all = lax.all_gather(grad_mlp_low, "tensor", axis=0, tiled=True)
    grad_down = jnp.einsum("rf,rd->fd", activated, grad_mlp_all, preferred_element_type=jnp.float32)
    grad_act = jnp.einsum("rd,fd->rf", grad_mlp_all, down_back, preferred_element_type=jnp.float32)
    unused_value, gelu_pull = jax.vjp(jax.nn.gelu, pre_act)
    grad_pre = gelu_pull(grad_act)[0].astype(jnp.bfloat16)
    grad_up = jnp.einsum("rd,rf->df", normed_all_two, grad_pre, preferred_element_type=jnp.float32)
    sum_up_local = jnp.sum(grad_pre.astype(jnp.float32), axis=0)
    norm_two_terms = jnp.einsum("rf,df->rd", grad_pre, up_back, preferred_element_type=jnp.float32)
    grad_norm_two = lax.psum_scatter(
        norm_two_terms.astype(jnp.bfloat16), "tensor", scatter_dimension=0, tiled=True
    ).astype(jnp.float32)
    unused_two, norm_two_pull = jax.vjp(layer_norm, hidden_one, ln2_gain, ln2_bias)
    back_hidden, grad_gain_two, grad_shift_two = norm_two_pull(grad_norm_two)
    grad_hidden = grad_top + back_hidden
    grad_attn_low = grad_hidden.astype(jnp.bfloat16)
    grad_attn_all = lax.all_gather(grad_attn_low, "tensor", axis=0, tiled=True)
    grad_outproj = jnp.einsum("re,rd->ed", mixed, grad_attn_all, preferred_element_type=jnp.float32)
    grad_mixed = jnp.einsum(
        "rd,ed->re", grad_attn_all, out_back, preferred_element_type=jnp.float32
    )
    grad_mixed = grad_mixed.astype(jnp.bfloat16).reshape(all_rows, heads_here, HD)

    def attend_backward(running, block_item):
        begin_row, log_total = block_item
        query_block, scores = block_scores(begin_row)
        weights_full = jnp.exp(scores - log_total[..., None])
        weights_low = weights_full.astype(jnp.bfloat16)
        grad_block = lax.dynamic_slice_in_dim(grad_mixed, begin_row, block_rows, 0)
        grad_weights = jnp.einsum(
            "qhd,khd->hqk", grad_block, values_all, preferred_element_type=jnp.float32
        )
        inner_sum = jnp.sum(weights_full * grad_weights, axis=-1, keepdims=True)
        grad_scores = (weights_full * (grad_weights - inner_sum)).astype(jnp.bfloat16)
        grad_query = (
            jnp.einsum("hqk,khd->qhd", grad_scores, keys_all, preferred_element_type=jnp.float32)
            * score_scale
        )
        key_acc, value_acc = running
        key_acc = (
            key_acc
            + jnp.einsum(
                "hqk,qhd->khd", grad_scores, query_block, preferred_element_type=jnp.float32
            )
            * score_scale
        )
        value_acc = value_acc + jnp.einsum(
            "hqk,qhd->khd", weights_low, grad_block, preferred_element_type=jnp.float32
        )
        return (
            (key_acc, value_acc),
            grad_query.astype(jnp.bfloat16).reshape(block_rows, head_cols),
        )

    zeros_acc = jnp.zeros((all_rows, heads_here, HD), jnp.float32)
    (key_acc, value_acc), grad_queries = lax.scan(
        attend_backward, (zeros_acc, zeros_acc), (block_starts, log_totals)
    )
    grad_projected = jnp.stack(
        [
            grad_queries.reshape(all_rows, head_cols),
            key_acc.reshape(all_rows, head_cols).astype(jnp.bfloat16),
            value_acc.reshape(all_rows, head_cols).astype(jnp.bfloat16),
        ]
    )
    grad_qkv = jnp.einsum(
        "rd,cre->cde", normed_all, grad_projected, preferred_element_type=jnp.float32
    )
    proj_sums = jnp.sum(grad_projected.astype(jnp.float32), axis=1)
    norm_one_terms = jnp.einsum(
        "cre,cde->rd", grad_projected, qkv_back, preferred_element_type=jnp.float32
    )
    grad_norm_one = lax.psum_scatter(
        norm_one_terms.astype(jnp.bfloat16), "tensor", scatter_dimension=0, tiled=True
    ).astype(jnp.float32)
    unused_one, norm_one_pull = jax.vjp(layer_norm, residual_in, ln1_gain, ln1_bias)
    back_input, grad_gain_one, grad_shift_one = norm_one_pull(grad_norm_one)
    grad_input = grad_hidden + back_input
    grad_qkv_out, grad_outproj_out, grad_up_out, grad_down_out = (
        lax.psum_scatter(grad_qkv, "dp", scatter_dimension=1, tiled=True),
        lax.psum_scatter(grad_outproj, "dp", scatter_dimension=1, tiled=True),
        lax.psum_scatter(grad_up, "dp", scatter_dimension=0, tiled=True),
        lax.psum_scatter(grad_down, "dp", scatter_dimension=1, tiled=True),
    )
    zero_index = jnp.zeros((), jnp.int32)
    qv_grad_full = lax.dynamic_update_slice(
        jnp.zeros((2, width), jnp.float32),
        jnp.stack([proj_sums[0], proj_sums[2]]),
        (zero_index, tensor_index * head_cols),
    )
    up_grad_full = lax.dynamic_update_slice(
        jnp.zeros((FF,), jnp.float32), sum_up_local, (tensor_index * hidden_cols,)
    )
    out_bias_local = jnp.sum(grad_attn_low.astype(jnp.float32), axis=0)
    down_bias_local = jnp.sum(grad_mlp_low.astype(jnp.float32), axis=0)
    small_sums = lax.psum(
        (
            grad_gain_one,
            grad_shift_one,
            qv_grad_full,
            out_bias_local,
            grad_gain_two,
            grad_shift_two,
            up_grad_full,
            down_bias_local,
        ),
        ("dp", "tensor"),
    )
    (
        sum_gain_one,
        sum_shift_one,
        sum_qv,
        sum_out_bias,
        sum_gain_two,
        sum_shift_two,
        sum_up_bias,
        sum_down_bias,
    ) = small_sums
    return (
        layer_out,
        grad_input,
        sum_gain_one,
        sum_shift_one,
        grad_qkv_out,
        sum_qv,
        grad_outproj_out,
        sum_out_bias,
        sum_gain_two,
        sum_shift_two,
        grad_up_out,
        sum_up_bias,
        grad_down_out,
        sum_down_bias,
    )


def solution(mesh):
    in_specs = (
        P(("dp", "tensor"), None),
        P("dp"),
        P(),
        P(),
        P(None, "dp", "tensor"),
        P(),
        P("tensor", "dp"),
        P(),
        P(),
        P(),
        P("dp", "tensor"),
        P(),
        P("tensor", "dp"),
        P(),
        P(("dp", "tensor"), None),
    )
    out_specs = (
        P(("dp", "tensor"), None),
        P(("dp", "tensor"), None),
        P(),
        P(),
        P(None, "dp", "tensor"),
        P(),
        P("tensor", "dp"),
        P(),
        P(),
        P(),
        P("dp", "tensor"),
        P(),
        P("tensor", "dp"),
        P(),
    )
    return jax.shard_map(shards, mesh=mesh, in_specs=in_specs, out_specs=out_specs, check_vma=False)
```

profile of v0, /device:TPU:1, one launch (start us, length us, event | category | flops | bytes accessed | tf_op | source)
XLA Modules:
  0.0 1102.5 jit_solution(16194078514107347193)
XLA Ops:
  14.5 26.1 %all_gather.30 = bf16[384,768]{0,1:T(8,128)(2,1)} all-gather(bf16[384,48]{0,1:T(8,128)(2,1)S(1)} %copy-done.26), channel_id=1, replica_groups=mesh['dp'=16,'tensor'=2] {'dp'}, dimensions={1}, use_global_device_ids=true | all-gather | bytes 626688 | tf_op jit(solution)/shard_map/all_gather | solution.py:54
  40.5 11.3 %all-gather.8.cloned.1.call-done = bf16[1536,768]{1,0:T(8,128)(2,1)} async-done(((bf16[768,768]{1,0:T(8,128)(2,1)}), bf16[1536,768]{1,0:T(8,128)(2,1)}) %all-gather.8.cloned.1.call-update) | async-done | bytes 2359312 | tf_op jit(solution)/shard_map/all_gather | solution.py:60
  51.8 43.2 %all-gather.10.cloned.1.call-done = bf16[3,768,384]{2,1,0:T(8,128)(2,1)} async-done(((bf16[3,48,384]{2,1,0:T(8,128)(2,1)}), bf16[3,768,384]{2,1,0:T(8,128)(2,1)}) %all-gather.10.cloned.1.call-update) | async-done | bytes 1769488 | tf_op jit(solution)/shard_map/all_gather | solution.py:53
  94.9 5.1 fusion.51
  102.9 67.5 %while.30 = (s32[]{:T(128)}, bf16[3,512,384]{2,1,0:T(8,128)(2,1)}, f32[3,6,512]{2,1,0:T(8,128)}, s32[3]{0:T(128)S(1)}, s32[]{:T(128)}, /*index=5*/bf16[1536,6,64...) while((s32[]{:T(128)}, bf16[3,512,384]{2,1,0:T(8,128)(2,1)}, ...), condition=%wide.region_5.6_spmd.clone.clone, body=%wide.region_2.5_spmd.clone.clone.sunk | while | flops 1266351104 | bytes 64597176 | solution.py:93
  107.4 4.8 fusion.134
  112.2 4.9 fusion.135
  117.1 6.7 fusion.136
  129.9 4.8 fusion.134
  134.7 4.9 fusion.135
  139.6 6.7 fusion.136
  152.4 4.8 fusion.134
  157.2 4.9 fusion.135
  162.1 6.7 fusion.136
  170.4 4.1 convolution_convert_fusion.2
  175.5 32.5 %reduce-scatter.8.cloned.1.call-done = bf16[768,768]{1,0:T(8,128)(2,1)} async-done(((bf16[1536,768]{1,0:T(8,128)(2,1)}), bf16[768,768]{1,0:T(8,128)(2,1)}) %reduce-scatter.8.cloned.1.call-update) | async-done | bytes 1179664 | tf_op jit(solution)/shard_map/reduce_scatter | solution.py:96
  213.6 3.2 convert_reduce_fusion.5
  219.0 34.0 %all-gather.14.cloned.1.call-done = bf16[768,1536]{1,0:T(8,128)(2,1)} async-done(((bf16[48,1536]{1,0:T(8,128)(2,1)}), bf16[768,1536]{1,0:T(8,128)(2,1)}) %all-gather.14.cloned.1.call-update) | async-done | bytes 2359312 | tf_op jit(solution)/shard_map/all_gather | solution.py:55
  253.0 36.5 %all-gather.12.cloned.1.call-done = bf16[1536,768]{1,0:T(8,128)(2,1)} async-done(((bf16[768,768]{1,0:T(8,128)(2,1)}), bf16[1536,768]{1,0:T(8,128)(2,1)}) %all-gather.12.cloned.1.call-update) | async-done | bytes 2359312 | tf_op jit(solution)/shard_map/all_gather | solution.py:101
  289.5 10.0 convolution_add_fusion
  299.5 28.1 %all-gather.18.cloned.1.call-done = bf16[1536,768]{1,0:T(8,128)(2,1)} async-done(((bf16[768,768]{1,0:T(8,128)(2,1)}), bf16[1536,768]{1,0:T(8,128)(2,1)}) %all-gather.18.cloned.1.call-update) | async-done | bytes 2359312 | tf_op jit(solution)/shard_map/all_gather | solution.py:118
  327.6 45.2 %all-gather.16.cloned.1.call-done = bf16[1536,768]{0,1:T(8,128)(2,1)} async-done(((bf16[1536,48]{0,1:T(8,128)(2,1)}), bf16[1536,768]{0,1:T(8,128)(2,1)}) %all-gather.16.cloned.1.call-update) | async-done | bytes 2359312 | tf_op jit(solution)/shard_map/all_gather | solution.py:56
  372.9 13.1 %convert_reduce_fusion = (f32[1536]{0:T(1024)}, bf16[1536,1536]{1,0:T(8,128)(2,1)S(1)}) fusion(f32[1536,1536]{1,0:T(8,128)} %convolution_add_fusion, bf16[1536,768]{1,0:T(8,128)(2,1)} %all-gather.18.cloned.1.call-done, bf16[1536,768]{0,1:T(8,128)(2,1)} %all-gather.16.cloned.1.call-done), kind=kOutput, calls=%fused_computation.60 | convolution fusion | flops 3675781632 | bytes 18880512 | tf_op jit(solution)/shard_map/rd,fd->rf/dot_general | solution.py:120
  388.1 5.1 convolution_convert_fusion
  393.2 9.9 convolution_convert_fusion.1
  403.2 23.2 %reduce-scatter.12.cloned.1.call-done = bf16[768,768]{1,0:T(8,128)(2,1)} async-done(((bf16[1536,768]{1,0:T(8,128)(2,1)}), bf16[768,768]{1,0:T(8,128)(2,1)}) %reduce-scatter.12.cloned.1.call-update) | async-done | bytes 1179664 | tf_op jit(solution)/shard_map/reduce_scatter | solution.py:126
  426.4 3.1 fusion.62
  430.1 33.3 %reduce-scatter.10.cloned.1.call-done = bf16[768,768]{1,0:T(8,128)(2,1)} async-done(((bf16[1536,768]{1,0:T(8,128)(2,1)}), bf16[768,768]{1,0:T(8,128)(2,1)}) %reduce-scatter.10.cloned.1.call-update) | async-done | bytes 1179664 | tf_op jit(solution)/shard_map/reduce_scatter | solution.py:106
  463.4 3.8 fusion.81
  469.7 36.2 %all-gather.20.cloned.1.call-done = bf16[1536,768]{1,0:T(8,128)(2,1)} async-done(((bf16[768,768]{1,0:T(8,128)(2,1)}), bf16[1536,768]{1,0:T(8,128)(2,1)}) %all-gather.20.cloned.1.call-update) | async-done | bytes 2359312 | tf_op jit(solution)/shard_map/all_gather | solution.py:133
  505.8 3.9 convolution_convert_fusion.3
  510.9 194.3 %while.31 = (s32[]{:T(128)}, f32[1536,6,64]{0,2,1:T(8,128)S(1)}, f32[1536,6,64]{0,2,1:T(8,128)}, bf16[3,512,384]{2,1,0:T(8,128)(2,1)}, s32[3]{0:T(128)S(1)}, /*i...) while((s32[]{:T(128)}, f32[1536,6,64]{0,2,1:T(8,128)S(1)}, ...), condition=%wide.region_15.16_spmd.clone.clone, body=%wide.region_13.15_spmd.clone.clone.sunk | while | flops 3095591936 | bytes 236809456 | solution.py:172
  525.2 3.8 fusion.146
  529.0 6.4 copy-done
  535.4 7.7 fusion.149
  543.2 14.6 %multiply_reduce_fusion.3 = (f32[6,512]{1,0:T(8,128)S(1)}, f32[6,512,1536]{2,1,0:T(8,128)}) fusion(f32[6,512,1536]{2,1,0:T(8,128)} %copy-done, f32[6,512]{1,0:T(8,128)S(1)} %dynamic-slice_bitcast_fusion.2, pred[512,1536]{1,0:T(8,128)(4,1)S(1)} %fusion.147, bf16[1536,6,64]{0,2,1:T(8,128)(2,1)} %get-tuple-element.553, ...), kind=kOutput, calls=%fused_computation.21.clone.1 | convolution fusion | flops 627569664 | bytes 40132612 | tf_op jit(solution)/shard_map/while/body/eval_jaxpr/qhd,khd->hqk/dot_general | solution.py:146
  557.7 13.2 %multiply_convert_fusion.5 = bf16[6,512,1536]{2,1,0:T(8,128)(2,1)S(1)} fusion(f32[6,512,1536]{2,1,0:T(8,128)} %get-tuple-element.480, f32[6,512,1536]{2,1,0:T(8,128)} %copy-done, f32[6,512]{1,0:T(8,128)S(1)} %get-tuple-element.481, f32[6,512]{1,0:T(8,128)S(1)} %dynamic-slice_bitcast_fusion.2, pred[512,1536]{1,0:T(8,128)(4,1)S(1)} %fusion.147), kind=kLoop, calls=%fused_computation.20.clone.1 | loop fusion | flops 28311552 | bytes 47996928 | tf_op jit(solution)/shard_map/while/body/eval_jaxpr/convert_element_type | solution.py:150
  571.0 3.7 fusion.150
  586.6 3.8 fusion.146
  590.4 6.4 copy-done
  596.8 8.2 fusion.149
  605.0 14.6 %multiply_reduce_fusion.3 = (f32[6,512]{1,0:T(8,128)S(1)}, f32[6,512,1536]{2,1,0:T(8,128)}) fusion(f32[6,512,1536]{2,1,0:T(8,128)} %copy-done, f32[6,512]{1,0:T(8,128)S(1)} %dynamic-slice_bitcast_fusion.2, pred[512,1536]{1,0:T(8,128)(4,1)S(1)} %fusion.147, bf16[1536,6,64]{0,2,1:T(8,128)(2,1)} %get-tuple-element.553, ...), kind=kOutput, calls=%fused_computation.21.clone.1 | convolution fusion | flops 627569664 | bytes 40132612 | tf_op jit(solution)/shard_map/while/body/eval_jaxpr/qhd,khd->hqk/dot_general | solution.py:146
  619.6 13.2 %multiply_convert_fusion.5 = bf16[6,512,1536]{2,1,0:T(8,128)(2,1)S(1)} fusion(f32[6,512,1536]{2,1,0:T(8,128)} %get-tuple-element.480, f32[6,512,1536]{2,1,0:T(8,128)} %copy-done, f32[6,512]{1,0:T(8,128)S(1)} %get-tuple-element.481, f32[6,512]{1,0:T(8,128)S(1)} %dynamic-slice_bitcast_fusion.2, pred[512,1536]{1,0:T(8,128)(4,1)S(1)} %fusion.147), kind=kLoop, calls=%fused_computation.20.clone.1 | loop fusion | flops 28311552 | bytes 47996928 | tf_op jit(solution)/shard_map/while/body/eval_jaxpr/convert_element_type | solution.py:150
  632.8 3.7 fusion.150
  636.6 3.0 fusion.148
  648.4 3.7 fusion.146
  652.2 6.4 copy-done
  658.7 8.2 fusion.149
  666.8 14.6 %multiply_reduce_fusion.3 = (f32[6,512]{1,0:T(8,128)S(1)}, f32[6,512,1536]{2,1,0:T(8,128)}) fusion(f32[6,512,1536]{2,1,0:T(8,128)} %copy-done, f32[6,512]{1,0:T(8,128)S(1)} %dynamic-slice_bitcast_fusion.2, pred[512,1536]{1,0:T(8,128)(4,1)S(1)} %fusion.147, bf16[1536,6,64]{0,2,1:T(8,128)(2,1)} %get-tuple-element.553, ...), kind=kOutput, calls=%fused_computation.21.clone.1 | convolution fusion | flops 627569664 | bytes 40132612 | tf_op jit(solution)/shard_map/while/body/eval_jaxpr/qhd,khd->hqk/dot_general | solution.py:146
  681.4 13.2 %multiply_convert_fusion.5 = bf16[6,512,1536]{2,1,0:T(8,128)(2,1)S(1)} fusion(f32[6,512,1536]{2,1,0:T(8,128)} %get-tuple-element.480, f32[6,512,1536]{2,1,0:T(8,128)} %copy-done, f32[6,512]{1,0:T(8,128)S(1)} %get-tuple-element.481, f32[6,512]{1,0:T(8,128)S(1)} %dynamic-slice_bitcast_fusion.2, pred[512,1536]{1,0:T(8,128)(4,1)S(1)} %fusion.147), kind=kLoop, calls=%fused_computation.20.clone.1 | loop fusion | flops 28311552 | bytes 47996928 | tf_op jit(solution)/shard_map/while/body/eval_jaxpr/convert_element_type | solution.py:150
  694.6 3.7 fusion.150
  708.7 6.8 fusion.68
  715.5 6.2 copy.45
  723.0 6.0 bitcast_convert_fusion
  729.1 9.1 fusion.85
  738.2 9.6 fusion.78
  756.2 81.8 %all-reduce.4.cloned.1.call-done = f32[3,768,384]{2,0,1:T(4,128)} async-done(((f32[3,768,384]{2,0,1:T(4,128)}), f32[3,768,384]{2,0,1:T(4,128)}) %all-reduce.4.cloned.1.call-update) | async-done | bytes 3538960
  839.7 36.4 %reduce-scatter.14.cloned.1.call-done = bf16[768,768]{1,0:T(8,128)(2,1)} async-done(((bf16[1536,768]{1,0:T(8,128)(2,1)}), bf16[768,768]{1,0:T(8,128)(2,1)}) %reduce-scatter.14.cloned.1.call-update) | async-done | bytes 1179664 | tf_op jit(solution)/shard_map/reduce_scatter | solution.py:189
  879.4 3.2 fusion.63
  882.7 42.8 %all-reduce.1 = (f32[768]{0:T(1024)}, f32[768]{0:T(1024)}, f32[2,768]{1,0:T(2,128)}, f32[768]{0:T(1024)}, f32[768]{0:T(1024)}, /*index=5*/f32[768]{0:T(1024)}, f32[3072]{0:T(1024)}, f32[768]{0:T(1024)}) all-reduce(f32[768]{0:T(1024)} %get-tuple-element.287, ...), channel_id=1, replica_groups=mesh['dp'=16,'tensor'=2] {'dp','tensor'}, use_global_device_ids=true, to_apply=%region_20.21 | all-reduce | flops 9216 | bytes 73728 | tf_op jit(solution)/shard_map/psum | solution.py:212
  926.1 3.6 add_add_fusion.2
  929.7 26.1 %reduce-scatter.18.cloned.1.call-done = f32[48,1536]{1,0:T(8,128)} async-done(((f32[768,1536]{1,0:T(8,128)}), f32[48,1536]{1,0:T(8,128)}) %reduce-scatter.18.cloned.1.call-update) | async-done | bytes 294928 | tf_op jit(solution)/shard_map/reduce_scatter | solution.py:198
  955.8 79.4 %reduce-scatter.20.cloned.1.call-done = f32[1536,48]{0,1:T(8,128)} async-done(((f32[1536,768]{0,1:T(8,128)}), f32[1536,48]{0,1:T(8,128)}) %reduce-scatter.20.cloned.1.call-update) | async-done | bytes 294928 | tf_op jit(solution)/shard_map/reduce_scatter | solution.py:199
  1035.1 60.4 %reduce-scatter.16.cloned.1.call-done = f32[384,48]{0,1:T(8,128)} async-done(((f32[384,768]{0,1:T(8,128)}), f32[384,48]{0,1:T(8,128)}) %reduce-scatter.16.cloned.1.call-update) | async-done | bytes 73744 | tf_op jit(solution)/shard_map/reduce_scatter | solution.py:197
  (193 shorter events, 81.3 us)
Async XLA Ops:
  7.2 4.7 copy-start.1
  7.2 4.7 copy-start.14
  7.2 4.7 copy-start.30
  7.2 44.5 %all-gather.8.cloned.1.call-start = ((), (), s32[]{:S(2)}) async-start(), calls=%async_computation.7 | async-start | bytes 3538944 | tf_op jit(solution)/shard_map/all_gather | solution.py:60
  8.8 2.4 copy-start.11
  8.9 5.4 copy-start.31
  8.9 5.6 copy-start.26
  10.7 0.6 copy-start.22
  11.3 0.6 copy-start.16
  13.4 81.5 %all-gather.10.cloned.1.call-start = ((), (), s32[]{:S(2)}) async-start(), calls=%async_computation.8 | async-start | bytes 1880064 | tf_op jit(solution)/shard_map/all_gather | solution.py:53
  14.2 193.8 %reduce-scatter.8.cloned.1.call-start = ((), (), s32[]{:S(2)}) async-start(), calls=%async_computation.9 | async-start | bytes 3538944 | tf_op jit(solution)/shard_map/reduce_scatter | solution.py:96
  102.9 67.5 %copy-start.10 = (bf16[384,768]{0,1:T(8,128)(2,1)S(1)}, bf16[384,768]{0,1:T(8,128)(2,1)}, u32[]{:S(2)}) copy-start(bf16[384,768]{0,1:T(8,128)(2,1)} %all_gather.30) | copy-start | bytes 1769476
  170.4 4.1 copy-start.35
  174.5 33.4 %copy-start.2 = (bf16[768,768]{1,0:T(8,128)(2,1)S(1)}, bf16[768,768]{1,0:T(8,128)(2,1)}, u32[]{:S(2)}) copy-start(bf16[768,768]{1,0:T(8,128)(2,1)} %param.19) | copy-start | bytes 3538948
  174.5 33.4 %copy-start.13 = (f32[768]{0:T(1024)S(1)}, f32[768]{0:T(1024)}, u32[]{:S(2)}) copy-start(f32[768]{0:T(1024)} %param.26) | copy-start | bytes 9220
  174.6 78.4 %all-gather.14.cloned.1.call-start = ((), (), s32[]{:S(2)}) async-start(), calls=%async_computation.11 | async-start | bytes 2506752 | tf_op jit(solution)/shard_map/all_gather | solution.py:55
  175.1 114.3 %all-gather.12.cloned.1.call-start = ((), (), s32[]{:S(2)}) async-start(), calls=%async_computation.10 | async-start | bytes 3538944 | tf_op jit(solution)/shard_map/all_gather | solution.py:101
  207.9 1.8 copy-start.4
  210.4 2.4 copy-start.24
  212.9 114.8 %all-gather.18.cloned.1.call-start = ((), (), s32[]{:S(2)}) async-start(), calls=%async_computation.14 | async-start | bytes 3538944 | tf_op jit(solution)/shard_map/all_gather | solution.py:118
  213.6 253.6 %copy-start.18 = (f32[768]{0:T(1024)}, f32[768]{0:T(1024)S(1)}, u32[]{:S(2)}) copy-start(f32[768]{0:T(1024)S(1)} %fusion.75) | copy-start | bytes 9220
  216.8 156.0 %all-gather.16.cloned.1.call-start = ((), (), s32[]{:S(2)}) async-start(), calls=%async_computation.12 | async-start | bytes 2506752 | tf_op jit(solution)/shard_map/all_gather | solution.py:56
  217.6 208.8 %reduce-scatter.12.cloned.1.call-start = ((), (), s32[]{:S(2)}) async-start(), calls=%async_computation.15 | async-start | bytes 3538944 | tf_op jit(solution)/shard_map/reduce_scatter | solution.py:126
  372.8 15.2 %copy-start.33 = (bf16[768,1536]{1,0:T(8,128)(2,1)S(1)}, bf16[768,1536]{1,0:T(8,128)(2,1)}, u32[]{:S(2)}) copy-start(bf16[768,1536]{1,0:T(8,128)(2,1)} %all-gather.14.cloned.1.call-done) | copy-start | bytes 7077892
  386.0 2.1 copy-start.37
  393.1 70.2 %reduce-scatter.10.cloned.1.call-start = ((), (), s32[]{:S(2)}) async-start(), calls=%async_computation.13 | async-start | bytes 3538944 | tf_op jit(solution)/shard_map/reduce_scatter | solution.py:106
  403.1 102.7 %all-gather.20.cloned.1.call-start = ((), (), s32[]{:S(2)}) async-start(), calls=%async_computation.16 | async-start | bytes 3538944 | tf_op jit(solution)/shard_map/all_gather | solution.py:133
  426.4 3.1 copy-start.25
  463.4 3.9 copy-start.7
  467.2 2.4 copy-start.5
  467.2 2.4 copy-start.27
  469.6 368.4 %all-reduce.4.cloned.1.call-start = ((), (), s32[]{:S(2)}) async-start(), calls=%async_computation.21 | async-start | bytes 9437184
  469.7 41.3 %copy-start.36 = (s32[3]{0:T(128)S(1)}, s32[3]{0:T(128)}, u32[]{:S(2)}) copy-start(s32[3]{0:T(128)} %copy-done.35) | copy-start | bytes 40
  529.0 6.5 copy-start
  590.4 6.5 copy-start
  652.2 6.5 copy-start
  721.7 1.3 copy-start.8
  721.8 154.4 %reduce-scatter.14.cloned.1.call-start = ((), (), s32[]{:S(2)}) async-start(), calls=%async_computation.17 | async-start | bytes 3538944 | tf_op jit(solution)/shard_map/reduce_scatter | solution.py:189
  729.0 226.7 %reduce-scatter.18.cloned.1.call-start = ((), (), s32[]{:S(2)}) async-start(), calls=%async_computation.19 | async-start | bytes 5013504 | tf_op jit(solution)/shard_map/reduce_scatter | solution.py:198
  738.1 297.0 %reduce-scatter.20.cloned.1.call-start = ((), (), s32[]{:S(2)}) async-start(), calls=%async_computation.20 | async-start | bytes 5013504 | tf_op jit(solution)/shard_map/reduce_scatter | solution.py:199
  747.8 0.7 copy-start.34
  747.8 347.7 %reduce-scatter.16.cloned.1.call-start = ((), (), s32[]{:S(2)}) async-start(), calls=%async_computation.18 | async-start | bytes 1253376 | tf_op jit(solution)/shard_map/reduce_scatter | solution.py:197
  750.9 0.6 copy-start.20
  751.5 1.3 copy-start.9
  751.5 2.1 copy-start.32
  753.6 2.5 copy-start.29
  753.6 122.5 %copy-start.12 = (f32[768]{0:T(1024)S(1)}, f32[768]{0:T(1024)}, u32[]{:S(2)}) copy-start(f32[768]{0:T(1024)} %copy-done.11) | copy-start | bytes 9220
  753.6 122.5 %copy-start.15 = (f32[768]{0:T(1024)S(1)}, f32[768]{0:T(1024)}, u32[]{:S(2)}) copy-start(f32[768]{0:T(1024)} %param.21) | copy-start | bytes 9220
  756.1 120.0 %copy-start.3 = (bf16[768,768]{1,0:T(8,128)(2,1)S(1)}, bf16[768,768]{1,0:T(8,128)(2,1)}, u32[]{:S(2)}) copy-start(bf16[768,768]{1,0:T(8,128)(2,1)} %param.19) | copy-start | bytes 3538948
  756.1 123.3 %copy-start.17 = (f32[768]{0:T(1024)S(1)}, f32[768]{0:T(1024)}, u32[]{:S(2)}) copy-start(f32[768]{0:T(1024)} %copy-done.16) | copy-start | bytes 9220
  756.2 82.8 %copy-start.28 = (f32[2,768]{1,0:T(2,128)}, f32[2,768]{1,0:T(2,128)S(1)}, u32[]{:S(2)}) copy-start(f32[2,768]{1,0:T(2,128)S(1)} %maximum_dynamic-update-slice_fusion) | copy-start | bytes 18436
  839.7 86.4 %copy-start.6 = (f32[768,768]{1,0:T(8,128)S(1)}, f32[768,768]{1,0:T(8,128)}, u32[]{:S(2)}) copy-start(f32[768,768]{1,0:T(8,128)} %copy-done.5) | copy-start | bytes 7077892
  839.7 86.4 %copy-start.19 = (f32[768]{0:T(1024)S(1)}, f32[768]{0:T(1024)}, u32[]{:S(2)}) copy-start(f32[768]{0:T(1024)} %copy-done.18) | copy-start | bytes 9220
  876.1 2.7 copy-start.23
  878.8 0.6 copy-start.21
Sparse Core Ops, SparseCore 0:
  13.5 38.1 all-gather.7
  54.1 40.8 all-gather.9
  174.7 33.1 reduce-scatter.7
  210.3 42.6 all-gather.13
  255.0 34.4 all-gather.11
  291.5 36.0 all-gather.17
  330.2 42.6 all-gather.15
  393.3 33.0 reduce-scatter.11
  428.6 34.7 reduce-scatter.9
  469.7 36.0 all-gather.19
  721.9 116.0 all-reduce.3
  840.7 35.3 reduce-scatter.13
  880.6 75.1 reduce-scatter.17
  960.5 74.5 reduce-scatter.19
  1039.2 56.2 reduce-scatter.15
where the time goes:
time: 1120 us; the launch traced here: 1100 us
  waiting for transfers between devices  610 us (54%)
  matrix products  219 us (20%)
  other arithmetic  104 us (9%)
  blocking collectives  68.8 us (6%)
  local copies, waits for them, and re-layouts  63.1 us (6%)
  loops' own time  21.3 us (2%)
  between operations  16 us (1%)
    unnamed x16, waiting for transfers between devices  83.9 us
    reduce_scatter x1, waiting for transfers between devices, shards(): lax.psum_scatter(grad_down, 'dp', scatter_dimension=1, tiled=True)  79.4 us
    reduce_scatter x1, waiting for transfers between devices, shards(): lax.psum_scatter(grad_outproj, 'dp', scatter_dimension=1, tiled=True)  60.4 us
    all_gather x1, waiting for transfers between devices, shards(): lax.all_gather(w_down, 'dp', axis=1, tiled=True)  45.2 us
    dot_general x3, matrix products, attend_backward(): jnp.einsum('qhd,khd->hqk', grad_block, values_all, preferred_element_type...  43.8 us
    all_gather x1, waiting for transfers between devices, shards(): lax.all_gather(w_qkv, 'dp', axis=1, tiled=True)  43.2 us
    psum x1, blocking collectives, shards(): lax.psum((grad_gain_one, grad_shift_one, qv_grad_full, out_bias_local, gr...  42.8 us
    convert_element_type x3, other arithmetic, attend_backward(): (weights_full * (grad_weights - inner_sum)).astype(jnp.bfloat16)  39.7 us
  transfers between devices with their start and end apart: 15, of which 15 were waited for; matrix products, arithmetic and copies ran while one was open for 7% of the time, Pallas kernels for 0%

commit v1 on v0

v1 whole, which is shorter than its diff:
```python
import functools
import math

import jax
import jax.numpy as jnp
from jax import lax
from jax.experimental import pallas as pl
from jax.experimental.pallas import tpu as pltpu
from jax.sharding import Mesh, PartitionSpec as P

HD = 64
LEN_MIN = 864
EPS = 1e-05
LANES = 128
BLOCK = 256
MASKED = -1000000000.0
F32 = jnp.float32
BF16 = jnp.bfloat16
NN = (((1,), (0,)), ((), ()))
NT = (((1,), (1,)), ((), ()))
TN = (((0,), (0,)), ((), ()))


def dot(left, right, dims=NN):
    return lax.dot_general(left, right, dims, preferred_element_type=F32)


def norm_stats(values):
    center = values - jnp.mean(values, axis=-1, keepdims=True)
    inverse = lax.rsqrt(jnp.mean(center * center, axis=-1, keepdims=True) + EPS)
    return center * inverse, inverse


def norm_back(grad, normed, inverse, gain):
    scaled = grad * gain
    back = inverse * (
        scaled
        - jnp.mean(scaled, axis=-1, keepdims=True)
        - normed * jnp.mean(scaled * normed, axis=-1, keepdims=True)
    )
    return back, jnp.sum(grad * normed, axis=0), jnp.sum(grad, axis=0)


def head_part(values, head):
    lane = lax.broadcasted_iota(jnp.int32, (1, LANES), 1)
    keep = (lane < HD) if head == 0 else (lane >= HD)
    return jnp.where(keep, values, jnp.zeros_like(values))


def lane_block(first):
    return pl.ds(pl.multiple_of(first, LANES), LANES)


def row_half(index, rows):
    return pl.ds(pl.multiple_of(index * rows, rows), rows)


def attend_forward_kernel(info, qkv_own, qkv_other, out_own, out_other, qkv, out):
    pair = pl.program_id(0)
    length, core = info[0], info[1]
    rows, width = qkv_own.shape[0], out_own.shape[1]
    blocks = 2 * rows // BLOCK

    @pl.when(pair == 0)
    def _():
        qkv[row_half(core, rows), :] = qkv_own[...]
        qkv[row_half(1 - core, rows), :] = qkv_other[...]

    first = pair * LANES

    def part(block, which):
        return qkv[block * BLOCK : (block + 1) * BLOCK, lane_block(which * width + first)]

    column = lax.broadcasted_iota(jnp.int32, (1, BLOCK), 1)
    row = lax.broadcasted_iota(jnp.int32, (BLOCK, 1), 0)

    def score(block, head):
        query = head_part(part(block, 0), head) * jnp.asarray(0.125, BF16)
        last = jnp.minimum(row + block * BLOCK, length - 1)
        scores = []
        for other in range(block + 1):
            piece = dot(query, part(other, 1), NT)
            if other == block or (other + 1) * BLOCK > LEN_MIN:
                piece = jnp.where(column + other * BLOCK <= last, piece, MASKED)
            scores.append(piece)
        return scores

    tasks = [(block, head) for block in range(blocks) for head in range(2)]
    upcoming = score(*tasks[0])
    kept = None
    for place, (block, head) in enumerate(tasks):
        scores = upcoming
        if place + 1 < len(tasks):
            upcoming = score(*tasks[place + 1])
        top = functools.reduce(jnp.maximum, scores)
        top = jnp.max(top, axis=1, keepdims=True)
        weights = [jnp.exp(piece - top) for piece in scores]
        total = jnp.sum(functools.reduce(jnp.add, weights), axis=1, keepdims=True)
        mixed = functools.reduce(
            jnp.add,
            [
                dot(weight.astype(BF16), head_part(part(other, 2), head))
                for other, weight in enumerate(weights)
            ],
        )
        mixed = mixed / total
        if head == 0:
            kept = mixed
        else:
            out[block * BLOCK : (block + 1) * BLOCK, lane_block(first)] = (kept + mixed).astype(BF16)

    @pl.when(pair == pl.num_programs(0) - 1)
    def _():
        out_own[...] = out[row_half(core, rows), :]
        out_other[...] = out[row_half(1 - core, rows), :]


def attend_forward(info, qkv_own, qkv_other):
    rows, width = qkv_own.shape[0], qkv_own.shape[1] // 3
    whole = pl.BlockSpec(memory_space=pltpu.VMEM)
    shape = jax.ShapeDtypeStruct((rows, width), BF16)
    return pl.pallas_call(
        attend_forward_kernel,
        grid=(width // LANES,),
        in_specs=[pl.BlockSpec(memory_space=pltpu.SMEM), whole, whole],
        out_specs=[whole, whole],
        out_shape=[shape, shape],
        scratch_shapes=[
            pltpu.VMEM((2 * rows, 3 * width), BF16),
            pltpu.VMEM((2 * rows, width), BF16),
        ],
        compiler_params=pltpu.CompilerParams(vmem_limit_bytes=48 * 1024 * 1024),
        name="attend_forward",
    )(info, qkv_own, qkv_other)


def attend_backward_kernel(
    info, qkv_own, qkv_other, grad_own, grad_other, back_own, back_other, qkv, grad, back, key_sum, value_sum
):
    pair = pl.program_id(0)
    length, core = info[0], info[1]
    rows, width = grad_own.shape
    blocks = 2 * rows // BLOCK

    @pl.when(pair == 0)
    def _():
        qkv[row_half(core, rows), :] = qkv_own[...]
        qkv[row_half(1 - core, rows), :] = qkv_other[...]
        grad[row_half(core, rows), :] = grad_own[...]
        grad[row_half(1 - core, rows), :] = grad_other[...]

    key_sum[...] = jnp.zeros_like(key_sum)
    value_sum[...] = jnp.zeros_like(value_sum)
    first = pair * LANES
    eighth = jnp.asarray(0.125, BF16)

    def span(block):
        return slice(block * BLOCK, (block + 1) * BLOCK)

    def part(block, which):
        return qkv[span(block), lane_block(which * width + first)]

    column = lax.broadcasted_iota(jnp.int32, (1, BLOCK), 1)
    row = lax.broadcasted_iota(jnp.int32, (BLOCK, 1), 0)

    def products(block, head):
        query = head_part(part(block, 0), head) * eighth
        mixed = head_part(grad[span(block), lane_block(first)], head)
        last = jnp.minimum(column + block * BLOCK, length - 1)
        scores, grads = [], []
        for other in range(block + 1):
            piece = dot(part(other, 1), query, NT)
            if other == block or (other + 1) * BLOCK > LEN_MIN:
                piece = jnp.where(row + other * BLOCK <= last, piece, MASKED)
            scores.append(piece)
            grads.append(dot(part(other, 2), mixed, NT))
        return query, mixed, scores, grads

    tasks = [(block, head) for block in range(blocks) for head in range(2)]
    upcoming = products(*tasks[0])
    kept = None
    for place, (block, head) in enumerate(tasks):
        query, mixed, scores, grads = upcoming
        if place + 1 < len(tasks):
            upcoming = products(*tasks[place + 1])
        top = jnp.max(functools.reduce(jnp.maximum, scores), axis=0, keepdims=True)
        weights = [jnp.exp(piece - top) for piece in scores]
        total = jnp.sum(functools.reduce(jnp.add, weights), axis=0, keepdims=True)
        inverse = 1.0 / total
        weights = [weight * inverse for weight in weights]
        products_sum = functools.reduce(jnp.add, [w * g for w, g in zip(weights, grads)])
        inner = jnp.sum(products_sum, axis=0, keepdims=True)
        query_sum = None
        for other in range(block + 1):
            weight = weights[other]
            change = (weight * (grads[other] - inner)).astype(BF16)
            value_sum[span(other), :] += dot(weight.astype(BF16), mixed)
            key_sum[span(other), :] += dot(change, query)
            piece = dot(change, head_part(part(other, 1), head) * eighth, TN)
            query_sum = piece if query_sum is None else query_sum + piece
        if head == 0:
            kept = query_sum
        else:
            back[span(block), lane_block(first)] = (kept + query_sum).astype(BF16)
    back[:, lane_block(width + first)] = key_sum[...].astype(BF16)
    back[:, lane_block(2 * width + first)] = value_sum[...].astype(BF16)

    @pl.when(pair == pl.num_programs(0) - 1)
    def _():
        back_own[...] = back[row_half(core, rows), :]
        back_other[...] = back[row_half(1 - core, rows), :]


def attend_backward(info, qkv_own, qkv_other, grad_own, grad_other):
    rows, width = grad_own.shape
    whole = pl.BlockSpec(memory_space=pltpu.VMEM)
    shape = jax.ShapeDtypeStruct((rows, 3 * width), BF16)
    return pl.pallas_call(
        attend_backward_kernel,
        grid=(width // LANES,),
        in_specs=[pl.BlockSpec(memory_space=pltpu.SMEM), whole, whole, whole, whole],
        out_specs=[whole, whole],
        out_shape=[shape, shape],
        scratch_shapes=[
            pltpu.VMEM((2 * rows, 3 * width), BF16),
            pltpu.VMEM((2 * rows, width), BF16),
            pltpu.VMEM((2 * rows, 3 * width), BF16),
            pltpu.VMEM((2 * rows, LANES), F32),
            pltpu.VMEM((2 * rows, LANES), F32),
        ],
        compiler_params=pltpu.CompilerParams(vmem_limit_bytes=48 * 1024 * 1024),
        name="attend_backward",
    )(info, qkv_own, qkv_other, grad_own, grad_other)


def swap(values):
    return lax.ppermute(values, ("core", "x"), [(0, 0), (1, 2), (2, 1), (3, 3)])


def exchange(values):
    return lax.ppermute(values, "core", [(0, 1), (1, 0)])


def gelu_parts(pre):
    slope = math.sqrt(2.0 / math.pi)
    bent = jnp.tanh(slope * (pre + 0.044715 * (pre * pre * pre)))
    value = 0.5 * pre * (1.0 + bent)
    change = 0.5 * (1.0 + bent) + 0.5 * pre * (1.0 - bent * bent) * slope * (1.0 + 3 * 0.044715 * pre * pre)
    return value, change


def shards(
    hidden_in,
    seq_lens,
    ln1_gain,
    ln1_bias,
    w_qkv,
    bias_qv,
    w_out,
    bias_out,
    ln2_gain,
    ln2_bias,
    w_up,
    bias_up,
    w_down,
    bias_down,
    grad_out,
):
    core = lax.axis_index("core")
    group = ("zy", "x")
    rows, width = hidden_in.shape
    shard_rows = w_up.shape[0]
    head_cols = w_qkv.shape[2]
    hidden_cols = w_up.shape[1]
    qkv_cols = 3 * head_cols

    residual_low = swap(hidden_in)
    length = swap(seq_lens)[0]
    attn_shard = swap(
        jnp.concatenate([w_qkv.transpose(1, 0, 2).reshape(shard_rows, qkv_cols), w_out.T], axis=1)
    )
    mlp_shard = swap(jnp.concatenate([w_up, w_down.T], axis=1))
    attn_weights = lax.all_gather(attn_shard, group, axis=0, tiled=True)
    mlp_weights = lax.all_gather(mlp_shard, group, axis=0, tiled=True)
    grad_low = swap(grad_out)

    qkv_weight, out_weight = attn_weights[:, :qkv_cols], attn_weights[:, qkv_cols:]
    up_weight, down_weight = mlp_weights[:, :hidden_cols], mlp_weights[:, hidden_cols:]
    info = jnp.stack([length, core.astype(jnp.int32)])

    residual = residual_low.astype(F32)
    unit_one, inverse_one = norm_stats(residual)
    norm_own = (unit_one * ln1_gain + ln1_bias).astype(BF16)
    norm_other = exchange(norm_own)
    bias_here = lax.dynamic_slice_in_dim(bias_qv, core * head_cols, head_cols, 1)
    qkv_bias = jnp.concatenate([bias_here[0], jnp.zeros((head_cols,), F32), bias_here[1]])
    qkv_own = (dot(norm_own, qkv_weight) + qkv_bias).astype(BF16)
    qkv_other = (dot(norm_other, qkv_weight) + qkv_bias).astype(BF16)
    mixed_own, mixed_other = attend_forward(info, qkv_own, qkv_other)
    attn_received = exchange(dot(mixed_other, out_weight, NT).astype(BF16))
    hidden = residual + (dot(mixed_own, out_weight, NT) + attn_received.astype(F32)) + bias_out
    unit_two, inverse_two = norm_stats(hidden)
    two_own = (unit_two * ln2_gain + ln2_bias).astype(BF16)
    two_other = exchange(two_own)
    bias_up_here = lax.dynamic_slice_in_dim(bias_up, core * hidden_cols, hidden_cols, 0)

    slots = core * rows + jnp.arange(rows, dtype=jnp.int32)
    grad_own = jnp.where((slots < length)[:, None], grad_low, jnp.zeros_like(grad_low))
    grad_other = exchange(grad_own)

    def feed(two, grad):
        pre = dot(two, up_weight) + bias_up_here
        value, change = gelu_parts(pre)
        active = value.astype(BF16)
        grad_pre = (dot(grad, down_weight) * change).astype(BF16)
        return active, grad_pre

    active_other, grad_pre_other = feed(two_other, grad_other)
    back_two_received = exchange(dot(grad_pre_other, up_weight, NT).astype(BF16))
    mlp_received = exchange(dot(active_other, down_weight, NT).astype(BF16))
    active_own, grad_pre_own = feed(two_own, grad_own)
    back_two = dot(grad_pre_own, up_weight, NT) + back_two_received.astype(F32)
    layer_out = hidden + (dot(active_own, down_weight, NT) + mlp_received.astype(F32)) + bias_down
    layer_out = swap(layer_out.astype(BF16))

    grad_up = dot(two_own, grad_pre_own, TN) + dot(two_other, grad_pre_other, TN)
    grad_down = dot(grad_own, active_own, TN) + dot(grad_other, active_other, TN)
    mlp_grads = jnp.concatenate([grad_up.astype(BF16), grad_down.astype(BF16)], axis=1)
    mlp_grads = swap(lax.psum_scatter(mlp_grads, group, scatter_dimension=0, tiled=True))

    back_hidden, gain_two_sum, shift_two_sum = norm_back(back_two, unit_two, inverse_two, ln2_gain)
    grad_hidden = grad_own.astype(F32) + back_hidden
    attn_grad_own = grad_hidden.astype(BF16)
    attn_grad_other = exchange(attn_grad_own)
    grad_mixed_own = dot(attn_grad_own, out_weight).astype(BF16)
    grad_mixed_other = dot(attn_grad_other, out_weight).astype(BF16)
    grad_outproj = dot(attn_grad_own, mixed_own, TN) + dot(attn_grad_other, mixed_other, TN)

    back_own, back_other = attend_backward(info, qkv_own, qkv_other, grad_mixed_own, grad_mixed_other)
    back_one_received = exchange(dot(back_other, qkv_weight, NT).astype(BF16))
    grad_qkv = dot(norm_own, back_own, TN) + dot(norm_other, back_other, TN)
    attn_grads = jnp.concatenate([grad_qkv.astype(BF16), grad_outproj.astype(BF16)], axis=1)
    attn_grads = swap(lax.psum_scatter(attn_grads, group, scatter_dimension=0, tiled=True))
    back_one = dot(back_own, qkv_weight, NT) + back_one_received.astype(F32)
    back_input, gain_one_sum, shift_one_sum = norm_back(back_one, unit_one, inverse_one, ln1_gain)
    grad_input = swap((grad_hidden + back_input).astype(BF16)).astype(F32)

    def place(values, full):
        return lax.dynamic_update_slice_in_dim(
            jnp.zeros(values.shape[:-1] + (full,), F32), values, core * values.shape[-1], values.ndim - 1
        )

    up_bias_sum = jnp.sum(grad_pre_own.astype(F32), axis=0) + jnp.sum(grad_pre_other.astype(F32), axis=0)
    back_sum = jnp.sum(back_own.astype(F32), axis=0) + jnp.sum(back_other.astype(F32), axis=0)
    qv_sum = jnp.stack([back_sum[:head_cols], back_sum[2 * head_cols :]])
    early = jnp.concatenate(
        [
            jnp.sum(grad_own.astype(F32), axis=0),
            gain_two_sum,
            shift_two_sum,
            jnp.sum(attn_grad_own.astype(F32), axis=0),
            place(up_bias_sum, bias_up.shape[0]),
        ]
    )
    late = jnp.concatenate([gain_one_sum, shift_one_sum, place(qv_sum, width).reshape(-1)])
    everyone = ("zy", "core", "x")
    early = lax.psum(early, everyone)
    late = lax.psum(late, everyone)
    down_bias, gain_two, shift_two, out_bias, up_bias = jnp.split(early, [width * n for n in range(1, 5)])
    gain_one, shift_one, qv_bias = jnp.split(late, [width, 2 * width])

    grad_w_qkv = attn_grads[:, :qkv_cols].reshape(shard_rows, 3, head_cols).transpose(1, 0, 2).astype(F32)
    grad_w_out = attn_grads[:, qkv_cols:].T.astype(F32)
    grad_w_up = mlp_grads[:, :hidden_cols].astype(F32)
    grad_w_down = mlp_grads[:, hidden_cols:].T.astype(F32)
    return (
        layer_out,
        grad_input,
        gain_one,
        shift_one,
        grad_w_qkv,
        qv_bias.reshape(2, width),
        grad_w_out,
        out_bias,
        gain_two,
        shift_two,
        grad_w_up,
        up_bias,
        grad_w_down,
        down_bias,
    )


def solution(mesh):
    cores = 2
    devices = mesh.devices
    inner = Mesh(devices.reshape(devices.shape[0] // cores, cores, devices.shape[1]), ("zy", "core", "x"))
    dp = ("zy", "core")
    token = P(("zy", "core", "x"), None)
    in_specs = (
        token,
        P(dp),
        P(),
        P(),
        P(None, dp, "x"),
        P(),
        P("x", dp),
        P(),
        P(),
        P(),
        P(dp, "x"),
        P(),
        P("x", dp),
        P(),
        token,
    )
    out_specs = (
        token,
        token,
        P(),
        P(),
        P(None, dp, "x"),
        P(),
        P("x", dp),
        P(),
        P(),
        P(),
        P(dp, "x"),
        P(),
        P("x", dp),
        P(),
    )
    return jax.shard_map(shards, mesh=inner, in_specs=in_specs, out_specs=out_specs, check_vma=False)
```

time: 1120 us -> 559 us (0.50)
  waiting for transfers between devices: 610 us -> 248 us
  matrix products: 219 us -> 82.4 us
  other arithmetic: 104 us -> 24 us
  Pallas kernels: 0 us -> 64.5 us
  starting transfers between devices: 0.87 us -> 46.5 us
  local copies, waits for them, and re-layouts: 63.1 us -> 18.6 us
  loops' own time: 21.3 us -> 0 us
  blocking collectives: 68.8 us -> 48.4 us
    all_gather x7 -> x2, waiting for transfers between devices: 234 us -> 57.6 us  [the longest x1 30.5 us: shards(): mlp_weights = lax.all_gather(mlp_shard, group, axis=0, tiled=True)]
    reduce_scatter x7 -> x2, waiting for transfers between devices: 291 us -> 150 us  [the longest x1 134 us: shards(): lax.psum_scatter(mlp_grads, group, scatter_dimension=0, tiled=True)]
    dot_general x33 -> x24, matrix products: 219 us -> 82.4 us  [dot(): return lax.dot_general(left, right, dims, preferred_element_type=F32)]
    unnamed x16 -> x4, waiting for transfers between devices: 83.9 us -> 0.07 us
    pallas_call x0 -> x2, Pallas kernels: none -> 64.5 us  [the longest x1 49.8 us: attend_backward(): pl.pallas_call(attend_backward_kernel, grid=(width // LANES,), in_specs=[...]
    ppermute x0 -> x17, starting transfers between devices: none -> 46.4 us  [the longest x9 35.4 us: swap(): return lax.ppermute(values, ('core', 'x'), [(0, 0), (1, 2), (2, 1), (3, 3)])]
    ppermute x0 -> x17, waiting for transfers between devices: none -> 40.9 us  [the longest x9 38.9 us: swap(): return lax.ppermute(values, ('core', 'x'), [(0, 0), (1, 2), (2, 1), (3, 3)])]
    convert_element_type x8 -> x6, other arithmetic: 45.5 us -> 7.12 us  [the longest x1 3.75 us: shards(): grad_input = swap((grad_hidden + back_input).astype(BF16)).astype(F32)]
  transfers between devices with their start and end apart: 15 -> 21, of which waited for: 15 -> 12; matrix products, arithmetic and copies ran while one was open for 7% -> 17% of each run, Pallas kernels for 0% -> 3%
where the time goes in v1:
time: 559 us; the launch traced here: 548 us
  waiting for transfers between devices  248 us (44%)
  matrix products  82.4 us (15%)
  Pallas kernels  64.5 us (12%)
  blocking collectives  48.4 us (9%)
  starting transfers between devices  46.5 us (8%)
  other arithmetic  24 us (4%)
  local copies, waits for them, and re-layouts  18.6 us (3%)
  between operations  15.3 us (3%)
    reduce_scatter x1, waiting for transfers between devices, shards(): lax.psum_scatter(mlp_grads, group, scatter_dimension=0, tiled=True)  134 us
    dot_general x24, matrix products, dot(): return lax.dot_general(left, right, dims, preferred_element_type=F32)  82.4 us
    pallas_call x1, Pallas kernels, attend_backward(): pl.pallas_call(attend_backward_kernel, grid=(width // LANES,), in_specs=[...  49.8 us
    psum x1, blocking collectives, shards(): late = lax.psum(late, everyone)  48.4 us
    ppermute x9, waiting for transfers between devices, swap(): return lax.ppermute(values, ('core', 'x'), [(0, 0), (1, 2), (2, 1), (3, 3)])  38.9 us
    ppermute x9, starting transfers between devices, swap(): return lax.ppermute(values, ('core', 'x'), [(0, 0), (1, 2), (2, 1), (3, 3)])  35.4 us
    all_gather x1, waiting for transfers between devices, shards(): mlp_weights = lax.all_gather(mlp_shard, group, axis=0, tiled=True)  30.5 us
    all_gather x1, waiting for transfers between devices, shards(): attn_weights = lax.all_gather(attn_shard, group, axis=0, tiled=True)  27.2 us
  transfers between devices with their start and end apart: 21, of which 12 were waited for; matrix products, arithmetic and copies ran while one was open for 17% of the time, Pallas kernels for 3%

profile of v1, /device:TPU:1, one launch (start us, length us, event | category | flops | bytes accessed | tf_op | source)
XLA Modules:
  0.0 548.0 jit_solution(5920648712374595679)
XLA Ops:
  7.2 1.0 copy.67
  9.0 4.5 collective-permute-start.2
  13.5 2.8 collective-permute-done.2
  17.1 1.0 pad_maximum_fusion.2
  18.1 3.6 collective-permute-start.5
  21.7 4.4 collective-permute-done.5
  27.6 3.6 collective-permute-start
  31.3 13.9 %collective-permute-done = bf16[768,768]{0,1:T(8,128)(2,1)S(1)} collective-permute-done((bf16[768,768]{0,1:T(8,128)(2,1)S(1)}, bf16[768,768]{0,1:T(8,128)(2,1)S(1)}, u32[]{:S(2)}, u32[]{:S(2)}) %collective-permute-start) | collective-permute-done | bytes 1179680 | tf_op jit(solution)/shard_map/ppermute | solution.py:237
  46.3 4.3 collective-permute-start.1
  50.7 1.6 collective-permute-done.1
  53.0 27.2 %all-gather.3.cloned.1.call-done = bf16[768,1536]{1,0:T(8,128)(2,1)} async-done(((bf16[48,1536]{1,0:T(8,128)(2,1)}), bf16[768,1536]{1,0:T(8,128)(2,1)}) %all-gather.3.cloned.1.call-update) | async-done | bytes 2359312 | tf_op jit(solution)/shard_map/all_gather | solution.py:283
  80.1 3.4 fusion.18.qkv_own
  83.5 3.6 fusion.19.qkv_other
  87.2 14.7 %attend_forward.1 = (bf16[768,384]{1,0:T(8,128)(2,1)S(1)}, bf16[768,384]{1,0:T(8,128)(2,1)S(1)}) custom-call(s32[2]{0:T(128)S(1)} %pad_add_fusion.info, bf16[768,1152]{1,0:T(8,128)(2,1)S(1)} %fusion.18.qkv_own, bf16[768,1152]{1,0:T(8,128)(2,1)S(1)} %fusion.19.qkv_other), custom_call_target="tpu_custom_call" | custom-call | tf_op jit(solution)/shard_map/attend_forward/pallas_call | solution.py:122
  102.0 0.8 copy-done.2
  102.8 0.8 copy-done.4
  103.6 1.8 convolution_convert_fusion.1
  105.4 1.3 collective-permute-start.4
  106.7 2.4 copy.48
  109.1 3.2 collective-permute-start.9
  112.3 1.0 copy-done.15
  113.3 2.7 fusion.62
  116.8 1.4 add_convert_fusion.3
  118.2 7.4 %collective-permute-start.6 = (bf16[768,768]{0,1:T(8,128)(2,1)}, bf16[768,768]{0,1:T(8,128)(2,1)}, u32[]{:S(2)}, u32[]{:S(2)}) collective-permute-start(bf16[768,768]{0,1:T(8,128)(2,1)} %add_convert_fusion.3), channel_id=1, source_target_pairs={{0,2},{2,0},{1,3},{3,1},{4,6},{6,4},{5,7},{7,5},{8,10},{10,8},{9,1... | collective-permute-start | bytes 3538952 | tf_op jit(solution)/shard_map/ppermute | solution.py:241
  126.2 7.0 %collective-permute-done.9 = bf16[768,768]{0,1:T(8,128)(2,1)} collective-permute-done((bf16[768,768]{0,1:T(8,128)(2,1)}, bf16[768,768]{0,1:T(8,128)(2,1)}, u32[]{:S(2)}, u32[]{:S(2)}) %collective-permute-start.9) | collective-permute-done | bytes 1179680 | tf_op jit(solution)/shard_map/ppermute | solution.py:237
  133.1 3.2 convert_reduce_fusion.5
  136.4 30.5 %all-gather.5.cloned.1.call-done = bf16[768,3072]{1,0:T(8,128)(2,1)} async-done(((bf16[48,3072]{1,0:T(8,128)(2,1)}), bf16[768,3072]{1,0:T(8,128)(2,1)}) %all-gather.5.cloned.1.call-update) | async-done | bytes 4718608 | tf_op jit(solution)/shard_map/all_gather | solution.py:284
  166.9 4.2 fusion.43
  171.1 7.7 %convert_reduce_fusion = (f32[1536]{0:T(1024)}, bf16[768,1536]{1,0:T(8,128)(2,1)S(1)}) fusion(f32[768,1536]{1,0:T(8,128)S(1)} %fusion.43, f32[1536]{0:T(1024)S(1)} %dynamic_slice.7, bf16[768,768]{0,1:T(8,128)(2,1)} %collective-permute-done.10, bf16[768,3072]{1,0:T(8,128)(2,1)S(1)} %copy-done.48), kind=kOutput, calls=%fused_computation.25 | convolution fusion | flops 1837890048 | bytes 10631168 | tf_op jit(solution)/shard_map/dot_general | solution.py:25
  178.8 2.0 convolution_convert_fusion.2
  180.9 1.6 collective-permute-start.11
  182.4 3.3 fusion.45
  185.8 7.7 %convert_reduce_fusion.1 = (f32[1536]{0:T(1024)}, bf16[768,1536]{1,0:T(8,128)(2,1)S(1)}) fusion(f32[768,1536]{1,0:T(8,128)S(1)} %fusion.45, f32[1536]{0:T(1024)S(1)} %dynamic_slice.7, bf16[768,768]{0,1:T(8,128)(2,1)} %get-tuple-element.65, bf16[768,3072]{1,0:T(8,128)(2,1)S(1)} %copy-done.48), kind=kOutput, calls=%fused_computation.26 | convolution fusion | flops 1837890048 | bytes 10631168 | tf_op jit(solution)/shard_map/dot_general | solution.py:25
  193.5 3.2 multiply_reduce_fusion
  196.8 3.8 convert_reduce_fusion.6
  201.4 2.0 collective-permute-done.12
  205.8 49.8 %attend_backward.1 = (bf16[768,1152]{1,0:T(8,128)(2,1)S(1)}, bf16[768,1152]{1,0:T(8,128)(2,1)S(1)}) custom-call(s32[2]{0:T(128)S(1)} %pad_add_fusion.info, bf16[768,1152]{1,0:T(8,128)(2,1)} %copy-done, bf16[768,1152]{1,0:T(8,128)(2,1)} %copy-done.1, bf16[768,384]{1,0:T(8,128)(2,1)S(1)} %convolution_convert_fusion.5.grad_own, ...), custom_call_target="tpu_custom_call" | custom-call | tf_op jit(solution)/shard_map/attend_backward/pallas_call | solution.py:218
  255.6 3.1 fusion.63
  258.7 1.7 fusion.20
  260.4 1.7 pad_maximum_fusion.1
  262.2 4.2 fusion.65
  266.4 3.4 add_convert_fusion.1
  269.8 3.5 fusion.57
  273.3 3.9 add_convert_fusion
  277.2 2.7 pad_maximum_fusion
  280.0 6.3 %convolution_convert_fusion.3 = bf16[768,768]{0,1:T(8,128)(2,1)} fusion(bf16[768,3072]{1,0:T(8,128)(2,1)} %all-gather.5.cloned.1.call-done, f32[768,1536]{1,0:T(8,128)} %copy-done.51, f32[1536]{0:T(1024)} %copy-done.36), kind=kOutput, calls=%fused_computation.73 | convolution fusion | flops 1824325632 | bytes 8265728 | tf_op jit(solution)/shard_map/dot_general | solution.py:25
  286.5 1.3 constant_dynamic-update-slice_fusion.4
  287.8 1.0 add_dynamic-update-slice_fusion
  288.9 3.4 convolution_convert_fusion
  292.8 7.0 %add_convert_fusion.2 = bf16[768,768]{0,1:T(8,128)(2,1)} fusion(f32[768,768]{0,1:T(8,128)S(1)} %copy-done.7, bf16[768,768]{0,1:T(8,128)(2,1)} %collective-permute-done.7, bf16[768,3072]{1,0:T(8,128)(2,1)} %all-gather.5.cloned.1.call-done, f32[768]{0:T(1024)S(1)} %copy-done.49, f32[768,1536]{1,0:T(8,128)} %copy-done.50, f32[1536]{0:T(1024)S(1)} %copy-done.38), kind=kOutput, calls=%fused_computation.64 | convolution fusion | flops 1826684928 | bytes 11805696 | tf_op jit(solution)/shard_map/dot_general | solution.py:25
  299.8 2.9 collective-permute-start.8
  302.9 3.0 fusion.34
  306.0 3.7 fusion.33
  309.8 2.6 collective-permute-start.14
  313.1 6.1 %collective-permute-done.8 = bf16[768,768]{0,1:T(8,128)(2,1)} collective-permute-done((bf16[768,768]{0,1:T(8,128)(2,1)}, bf16[768,768]{0,1:T(8,128)(2,1)}, u32[]{:S(2)}, u32[]{:S(2)}) %collective-permute-start.8) | collective-permute-done | bytes 1179680 | tf_op jit(solution)/shard_map/ppermute | solution.py:237
  319.2 2.4 copy.55
  321.6 48.4 %all-reduce = (f32[3072]{0:T(1024)S(1)}, f32[6144]{0:T(1024)S(1)}) all-reduce(f32[3072]{0:T(1024)S(1)} %pad_maximum_fusion.4, f32[6144]{0:T(1024)S(1)} %copy-done.31), channel_id=1, replica_groups=mesh['zy'=8,'core'=2,'x'=2] {'zy','core','x'}, use_global_device_ids=true, to_apply=%region_12.13 | all-reduce | flops 9216 | bytes 73728 | tf_op jit(solution)/shard_map/psum | solution.py:368
  371.8 15.8 %reduce-scatter.3.cloned.1.call-done = bf16[48,1536]{1,0:T(8,128)(2,1)} async-done(((bf16[768,1536]{1,0:T(8,128)(2,1)}), bf16[48,1536]{1,0:T(8,128)(2,1)}) %reduce-scatter.3.cloned.1.call-update) | async-done | bytes 147472 | tf_op jit(solution)/shard_map/reduce_scatter | solution.py:343
  387.6 5.2 collective-permute-start.15
  393.4 2.7 copy.56
  396.1 134.0 %reduce-scatter.5.cloned.1.call-done = bf16[48,3072]{1,0:T(8,128)(2,1)} async-done(((bf16[768,3072]{1,0:T(8,128)(2,1)}), bf16[48,3072]{1,0:T(8,128)(2,1)}) %reduce-scatter.5.cloned.1.call-update) | async-done | bytes 294928 | tf_op jit(solution)/shard_map/reduce_scatter | solution.py:329
  530.1 5.4 collective-permute-start.16
  537.0 3.1 collective-permute-done.16
  540.1 0.9 convert_bitcast_fusion
  (187 shorter events, 14.9 us)
Async XLA Ops:
  7.2 19.8 %copy-start.12 = (bf16[768,768]{1,0:T(8,128)(2,1)S(1)}, bf16[768,768]{1,0:T(8,128)(2,1)}, u32[]{:S(2)}) copy-start(bf16[768,768]{1,0:T(8,128)(2,1)} %param.15) | copy-start | bytes 3538948
  7.2 72.9 %all-gather.3.cloned.1.call-start = ((), (), s32[]{:S(2)}) async-start(), calls=%async_computation.2 | async-start | bytes 2506752 | tf_op jit(solution)/shard_map/all_gather | solution.py:283
  9.0 7.3 %collective-permute-start.2 = (bf16[48,1536]{1,0:T(8,128)(2,1)S(1)}, bf16[48,1536]{1,0:T(8,128)(2,1)S(1)}, u32[]{:S(2)}, u32[]{:S(2)}) collective-permute-start(bf16[48,1536]{1,0:T(8,128)(2,1)S(1)} %pad_maximum_fusion.3), channel_id=1, source_target_pairs={{0,0},{1,2},{2,1},{3,3},{4,4},{5,6},{6,5},{7,7},{8,8},{9,10},{10,9... | collective-permute-start | bytes 442376 | tf_op jit(solution)/shard_map/ppermute | solution.py:237
  17.0 149.8 %all-gather.5.cloned.1.call-start = ((), (), s32[]{:S(2)}) async-start(), calls=%async_computation.3 | async-start | bytes 5013504 | tf_op jit(solution)/shard_map/all_gather | solution.py:284
  18.1 8.0 %collective-permute-start.5 = (bf16[48,3072]{1,0:T(8,128)(2,1)S(1)}, bf16[48,3072]{1,0:T(8,128)(2,1)S(1)}, u32[]{:S(2)}, u32[]{:S(2)}) collective-permute-start(bf16[48,3072]{1,0:T(8,128)(2,1)S(1)} %pad_maximum_fusion.2), channel_id=1, source_target_pairs={{0,0},{1,2},{2,1},{3,3},{4,4},{5,6},{6,5},{7,7},{8,8},{9,10},{10,9... | collective-permute-start | bytes 884744 | tf_op jit(solution)/shard_map/ppermute | solution.py:237
  26.9 18.9 %copy-start.32 = (f32[768]{0:T(1024)S(1)}, f32[768]{0:T(1024)}, u32[]{:S(2)}) copy-start(f32[768]{0:T(1024)} %param.17) | copy-start | bytes 9220
  26.9 18.9 %copy-start.40 = (f32[768]{0:T(1024)S(1)}, f32[768]{0:T(1024)}, u32[]{:S(2)}) copy-start(f32[768]{0:T(1024)} %param.18) | copy-start | bytes 9220
  26.9 360.7 %reduce-scatter.3.cloned.1.call-start = ((), (), s32[]{:S(2)}) async-start(), calls=%async_computation.4 | async-start | bytes 2506752 | tf_op jit(solution)/shard_map/reduce_scatter | solution.py:343
  27.6 23.0 %copy-start.47 = (f32[2,768]{1,0:T(2,128)S(1)}, f32[2,768]{1,0:T(2,128)}, u32[]{:S(2)}) copy-start(f32[2,768]{1,0:T(2,128)} %param.20) | copy-start | bytes 18436
  27.6 17.5 %collective-permute-start = (bf16[768,768]{0,1:T(8,128)(2,1)S(1)}, bf16[768,768]{0,1:T(8,128)(2,1)S(1)}, u32[]{:S(2)}, u32[]{:S(2)}) collective-permute-start(bf16[768,768]{0,1:T(8,128)(2,1)S(1)} %copy.43), channel_id=1, source_target_pairs={{0,0},{1,2},{2,1},{3,3},{4,4},{5,6},{6,5},{7,7},{8,8},{9,10},{10,9... | collective-permute-start | bytes 3538952 | tf_op jit(solution)/shard_map/ppermute | solution.py:237
  45.8 37.7 %copy-start.23 = (f32[768]{0:T(1024)}, f32[768]{0:T(1024)S(1)}, u32[]{:S(2)}) copy-start(f32[768]{0:T(1024)S(1)} %add_rsqrt_fusion.1) | copy-start | bytes 9220
  46.2 37.3 %copy-start.13 = (bf16[768,768]{0,1:T(8,128)(2,1)}, bf16[768,768]{0,1:T(8,128)(2,1)S(1)}, u32[]{:S(2)}) copy-start(bf16[768,768]{0,1:T(8,128)(2,1)S(1)} %fusion.28) | copy-start | bytes 3538948
  46.2 37.3 %collective-permute-start.3 = (bf16[768,768]{0,1:T(8,128)(2,1)S(1)}, bf16[768,768]{0,1:T(8,128)(2,1)}, u32[]{:S(2)}, u32[]{:S(2)}) collective-permute-start(bf16[768,768]{0,1:T(8,128)(2,1)S(1)} %fusion.28), channel_id=1, source_target_pairs={{0,2},{2,0},{1,3},{3,1},{4,6},{6,4},{5,7},{7,5},{8,10},{10,8},{9,1... | collective-permute-start | bytes 3538952 | tf_op jit(solution)/shard_map/ppermute | solution.py:241
  46.3 6.0 %collective-permute-start.1 = (s32[1]{0:T(128)}, s32[1]{0:T(128)}, u32[]{:S(2)}, u32[]{:S(2)}) collective-permute-start(s32[1]{0:T(128)} %param.16), channel_id=1, source_target_pairs={{0,0},{1,2},{2,1},{3,3},{4,4},{5,6},{6,5},{7,7},{8,8},{9,10},{10,9... | collective-permute-start | bytes 20 | tf_op jit(solution)/shard_map/ppermute | solution.py:237
  80.1 3.4 copy-start.17
  83.5 3.7 copy-start
  87.2 18.2 %copy-start.1 = (bf16[768,1152]{1,0:T(8,128)(2,1)}, bf16[768,1152]{1,0:T(8,128)(2,1)S(1)}, u32[]{:S(2)}) copy-start(bf16[768,1152]{1,0:T(8,128)(2,1)S(1)} %fusion.19.qkv_other) | copy-start | bytes 5308420
  103.6 9.7 %copy-start.3 = (bf16[768,384]{1,0:T(8,128)(2,1)S(1)}, bf16[768,384]{1,0:T(8,128)(2,1)}, u32[]{:S(2)}) copy-start(bf16[768,384]{1,0:T(8,128)(2,1)} %copy-done.2) | copy-start | bytes 1769476
  103.6 9.7 %copy-start.46 = (f32[768]{0:T(1024)S(1)}, f32[768]{0:T(1024)}, u32[]{:S(2)}) copy-start(f32[768]{0:T(1024)} %param.22) | copy-start | bytes 9220
  105.4 6.9 %collective-permute-start.4 = (bf16[768,768]{0,1:T(8,128)(2,1)}, bf16[768,768]{0,1:T(8,128)(2,1)S(1)}, u32[]{:S(2)}, u32[]{:S(2)}) collective-permute-start(bf16[768,768]{0,1:T(8,128)(2,1)} %convolution_convert_fusion.1), channel_id=1, source_target_pairs={{0,2},{2,0},{1,3},{3,1},{4,6},{6,4},{5,7},{7,5},{8,10},{10,8},{9,1... | collective-permute-start | bytes 3538952 | tf_op jit(solution)/shard_map/ppermute | solution.py:241
  109.1 24.0 %collective-permute-start.9 = (bf16[768,768]{0,1:T(8,128)(2,1)}, bf16[768,768]{0,1:T(8,128)(2,1)}, u32[]{:S(2)}, u32[]{:S(2)}) collective-permute-start(bf16[768,768]{0,1:T(8,128)(2,1)} %copy.48), channel_id=1, source_target_pairs={{0,0},{1,2},{2,1},{3,3},{4,4},{5,6},{6,5},{7,7},{8,8},{9,10},{10,9... | collective-permute-start | bytes 3538952 | tf_op jit(solution)/shard_map/ppermute | solution.py:237
  116.0 80.7 %copy-start.6 = (f32[768,768]{0,1:T(8,128)}, f32[768,768]{0,1:T(8,128)S(1)}, u32[]{:S(2)}) copy-start(f32[768,768]{0,1:T(8,128)S(1)} %get-tuple-element.77) | copy-start | bytes 7077892
  116.8 19.5 %copy-start.39 = (f32[3072]{0:T(1024)S(1)}, f32[3072]{0:T(1024)}, u32[]{:S(2)}) copy-start(f32[3072]{0:T(1024)} %param.26) | copy-start | bytes 36868
  118.2 18.2 %collective-permute-start.6 = (bf16[768,768]{0,1:T(8,128)(2,1)}, bf16[768,768]{0,1:T(8,128)(2,1)}, u32[]{:S(2)}, u32[]{:S(2)}) collective-permute-start(bf16[768,768]{0,1:T(8,128)(2,1)} %add_convert_fusion.3), channel_id=1, source_target_pairs={{0,2},{2,0},{1,3},{3,1},{4,6},{6,4},{5,7},{7,5},{8,10},{10,8},{9,1... | collective-permute-start | bytes 3538952 | tf_op jit(solution)/shard_map/ppermute | solution.py:241
  136.3 34.8 %collective-permute-start.10 = (bf16[768,768]{0,1:T(8,128)(2,1)}, bf16[768,768]{0,1:T(8,128)(2,1)}, u32[]{:S(2)}, u32[]{:S(2)}) collective-permute-start(bf16[768,768]{0,1:T(8,128)(2,1)} %get-tuple-element.65), channel_id=1, source_target_pairs={{0,2},{2,0},{1,3},{3,1},{4,6},{6,4},{5,7},{7,5},{8,10},{10,8},{9,1... | collective-permute-start | bytes 3538952 | tf_op jit(solution)/shard_map/ppermute | solution.py:241
  136.4 49.4 %copy-start.36 = (f32[1536]{0:T(1024)}, f32[1536]{0:T(1024)S(1)}, u32[]{:S(2)}) copy-start(f32[1536]{0:T(1024)S(1)} %dynamic_slice.7) | copy-start | bytes 18436
  166.8 4.2 copy-start.48
  171.1 7.8 %copy-start.51 = (f32[768,1536]{1,0:T(8,128)}, f32[768,1536]{1,0:T(8,128)S(1)}, u32[]{:S(2)}) copy-start(f32[768,1536]{1,0:T(8,128)S(1)} %fusion.43) | copy-start | bytes 14155780
  180.9 12.6 %collective-permute-start.11 = (bf16[768,768]{0,1:T(8,128)(2,1)S(1)}, bf16[768,768]{0,1:T(8,128)(2,1)S(1)}, u32[]{:S(2)}, u32[]{:S(2)}) collective-permute-start(bf16[768,768]{0,1:T(8,128)(2,1)S(1)} %convolution_convert_fusion.2), channel_id=1, source_target_pairs={{0,2},{2,0},{1,3},{3,1},{4,6},{6,4},{5,7},{7,5},{8,10},{10,8},{9,1... | collective-permute-start | bytes 3538952 | tf_op jit(solution)/shard_map/ppermute | solution.py:241
  185.8 7.8 %copy-start.50 = (f32[768,1536]{1,0:T(8,128)}, f32[768,1536]{1,0:T(8,128)S(1)}, u32[]{:S(2)}) copy-start(f32[768,1536]{1,0:T(8,128)S(1)} %fusion.45) | copy-start | bytes 14155780
  193.5 3.2 copy-start.52
  196.7 3.8 copy-start.10
  196.7 3.8 copy-start.25
  196.7 3.8 copy-start.27
  196.8 3.9 copy-start.18
  200.5 2.9 collective-permute-start.12
  262.1 268.0 %reduce-scatter.5.cloned.1.call-start = ((), (), s32[]{:S(2)}) async-start(), calls=%async_computation.5 | async-start | bytes 5013504 | tf_op jit(solution)/shard_map/reduce_scatter | solution.py:329
  262.1 4.2 copy-start.54
  262.2 7.6 %slice-start.2 = ((s8[4718592]{0:T(1024)(128)(4,1)}), s8[4194304]{0:T(1024)(128)(4,1)S(1)}, s32[]{:S(2)}) async-start(s8[4718592]{0:T(1024)(128)(4,1)} %bitcast.47), calls=%async_computation.8 | async-start | bytes 8388608
  262.2 11.1 %slice-start = ((s8[4718592]{0:T(1024)(128)(4,1)}), s8[4194304]{0:T(1024)(128)(4,1)S(1)}, s32[]{:S(2)}) async-start(s8[4718592]{0:T(1024)(128)(4,1)} %bitcast.45), calls=%async_computation.6 | async-start | bytes 8388608
  266.3 3.4 copy-start.37
  266.4 3.4 slice-start.3
  266.4 6.9 %slice-start.1 = ((s8[4718592]{0:T(1024)(128)(4,1)}), s8[524288]{0:T(1024)(128)(4,1)S(1)}, s32[]{:S(2)}) async-start(s8[4718592]{0:T(1024)(128)(4,1)} %bitcast.45), calls=%async_computation.7 | async-start | bytes 1048576
  280.0 6.5 %copy-start.34 = (f32[768]{0:T(1024)S(1)}, f32[768]{0:T(1024)}, u32[]{:S(2)}) copy-start(f32[768]{0:T(1024)} %get-tuple-element.64) | copy-start | bytes 9220
  286.3 6.4 %collective-permute-start.7 = (bf16[768,768]{0,1:T(8,128)(2,1)}, bf16[768,768]{0,1:T(8,128)(2,1)}, u32[]{:S(2)}, u32[]{:S(2)}) collective-permute-start(bf16[768,768]{0,1:T(8,128)(2,1)} %convolution_convert_fusion.3), channel_id=1, source_target_pairs={{0,2},{2,0},{1,3},{3,1},{4,6},{6,4},{5,7},{7,5},{8,10},{10,8},{9,1... | collective-permute-start | bytes 3538952 | tf_op jit(solution)/shard_map/ppermute | solution.py:241
  288.9 3.9 copy-start.7
  288.9 3.9 copy-start.38
  288.9 3.9 copy-start.49
  292.3 10.5 %copy-start.29 = (f32[6144]{0:T(1024)S(1)}, f32[6144]{0:T(1024)}, u32[]{:S(2)}) copy-start(f32[6144]{0:T(1024)} %constant_dynamic-update-slice_fusion.4) | copy-start | bytes 73732
  292.3 10.5 %copy-start.45 = (f32[768]{0:T(1024)S(1)}, f32[768]{0:T(1024)}, u32[]{:S(2)}) copy-start(f32[768]{0:T(1024)} %get-tuple-element.50) | copy-start | bytes 9220
  292.3 10.5 %copy-start.44 = (f32[768]{0:T(1024)S(1)}, f32[768]{0:T(1024)}, u32[]{:S(2)}) copy-start(f32[768]{0:T(1024)} %get-tuple-element.56) | copy-start | bytes 9220
  292.3 10.5 %copy-start.35 = (f32[768]{0:T(1024)S(1)}, f32[768]{0:T(1024)}, u32[]{:S(2)}) copy-start(f32[768]{0:T(1024)} %get-tuple-element.62) | copy-start | bytes 9220
  292.3 10.6 %copy-start.9 = (bf16[768,768]{0,1:T(8,128)(2,1)S(1)}, bf16[768,768]{0,1:T(8,128)(2,1)}, u32[]{:S(2)}) copy-start(bf16[768,768]{0,1:T(8,128)(2,1)} %copy-done.8) | copy-start | bytes 3538948
  292.3 10.6 %copy-start.19 = (bf16[768,1536]{1,0:T(8,128)(2,1)S(1)}, bf16[768,1536]{1,0:T(8,128)(2,1)}, u32[]{:S(2)}) copy-start(bf16[768,1536]{1,0:T(8,128)(2,1)} %all-gather.3.cloned.1.call-done) | copy-start | bytes 7077892
  292.3 10.6 %copy-start.24 = (f32[768]{0:T(1024)S(1)}, f32[768]{0:T(1024)}, u32[]{:S(2)}) copy-start(f32[768]{0:T(1024)} %copy-done.23) | copy-start | bytes 9220
  292.4 10.6 %copy-start.33 = (f32[768]{0:T(1024)S(1)}, f32[768]{0:T(1024)}, u32[]{:S(2)}) copy-start(f32[768]{0:T(1024)} %param.17) | copy-start | bytes 9220
  292.4 10.5 %collective-permute-start.13 = (bf16[768,768]{0,1:T(8,128)(2,1)S(1)}, bf16[768,768]{0,1:T(8,128)(2,1)S(1)}, u32[]{:S(2)}, u32[]{:S(2)}) collective-permute-start(bf16[768,768]{0,1:T(8,128)(2,1)S(1)} %convolution_convert_fusion), channel_id=1, source_target_pairs={{0,2},{2,0},{1,3},{3,1},{4,6},{6,4},{5,7},{7,5},{8,10},{10,8},{9,1... | collective-permute-start | bytes 3538952 | tf_op jit(solution)/shard_map/ppermute | solution.py:241
  299.8 19.4 %collective-permute-start.8 = (bf16[768,768]{0,1:T(8,128)(2,1)}, bf16[768,768]{0,1:T(8,128)(2,1)}, u32[]{:S(2)}, u32[]{:S(2)}) collective-permute-start(bf16[768,768]{0,1:T(8,128)(2,1)} %add_convert_fusion.2), channel_id=1, source_target_pairs={{0,0},{1,2},{2,1},{3,3},{4,4},{5,6},{6,5},{7,7},{8,8},{9,10},{10,9... | collective-permute-start | bytes 3538952 | tf_op jit(solution)/shard_map/ppermute | solution.py:237
  309.8 83.7 %collective-permute-start.14 = (bf16[768,768]{0,1:T(8,128)(2,1)}, bf16[768,768]{0,1:T(8,128)(2,1)}, u32[]{:S(2)}, u32[]{:S(2)}) collective-permute-start(bf16[768,768]{0,1:T(8,128)(2,1)} %fusion.33), channel_id=1, source_target_pairs={{0,0},{1,2},{2,1},{3,3},{4,4},{5,6},{6,5},{7,7},{8,8},{9,10},{10,9... | collective-permute-start | bytes 3538952 | tf_op jit(solution)/shard_map/ppermute | solution.py:237
  312.7 8.9 %copy-start.42 = (f32[768]{0:T(1024)S(1)}, f32[768]{0:T(1024)}, u32[]{:S(2)}) copy-start(f32[768]{0:T(1024)} %get-tuple-element.52) | copy-start | bytes 9220
  312.7 8.9 %copy-start.43 = (f32[768]{0:T(1024)S(1)}, f32[768]{0:T(1024)}, u32[]{:S(2)}) copy-start(f32[768]{0:T(1024)} %get-tuple-element.57) | copy-start | bytes 9220
  312.7 8.9 %copy-start.31 = (f32[6144]{0:T(1024)S(1)}, f32[6144]{0:T(1024)}, u32[]{:S(2)}) copy-start(f32[6144]{0:T(1024)} %copy-done.30) | copy-start | bytes 73732
  387.6 147.9 %collective-permute-start.15 = (bf16[48,1536]{1,0:T(8,128)(2,1)}, bf16[48,1536]{1,0:T(8,128)(2,1)S(1)}, u32[]{:S(2)}, u32[]{:S(2)}) collective-permute-start(bf16[48,1536]{1,0:T(8,128)(2,1)} %reduce-scatter.3.cloned.1.call-done), channel_id=1, source_target_pairs={{0,0},{1,2},{2,1},{3,3},{4,4},{5,6},{6,5},{7,7},{8,8},{9,10},{10,9... | collective-permute-start | bytes 442376 | tf_op jit(solution)/shard_map/ppermute | solution.py:237
  530.1 10.0 %collective-permute-start.16 = (bf16[48,3072]{1,0:T(8,128)(2,1)}, bf16[48,3072]{1,0:T(8,128)(2,1)S(1)}, u32[]{:S(2)}, u32[]{:S(2)}) collective-permute-start(bf16[48,3072]{1,0:T(8,128)(2,1)} %reduce-scatter.5.cloned.1.call-done), channel_id=1, source_target_pairs={{0,0},{1,2},{2,1},{3,3},{4,4},{5,6},{6,5},{7,7},{8,8},{9,10},{10,9... | collective-permute-start | bytes 884744 | tf_op jit(solution)/shard_map/ppermute | solution.py:237
  (16 other events, 30.3 us)
Sparse Core Ops, SparseCore 0:
  17.2 62.9 all-gather.2
  83.5 83.3 all-gather.4
  262.2 125.3 reduce-scatter.2
  393.5 136.6 reduce-scatter.4

commit v2 on v1

v2 whole, which is shorter than its diff:
```python
import functools
import math

import jax
import jax.numpy as jnp
from jax import lax
from jax.experimental import pallas as pl
from jax.experimental.pallas import tpu as pltpu
from jax.sharding import Mesh, PartitionSpec as P

HD = 64
LEN_MIN = 864
EPS = 1e-05
LANES = 128
BLOCK = 256
MASKED = -1000000000.0
F32 = jnp.float32
BF16 = jnp.bfloat16
NN = (((1,), (0,)), ((), ()))
NT = (((1,), (1,)), ((), ()))
TN = (((0,), (0,)), ((), ()))


def dot(left, right, dims=NN):
    return lax.dot_general(left, right, dims, preferred_element_type=F32)


def norm_stats(values):
    center = values - jnp.mean(values, axis=-1, keepdims=True)
    inverse = lax.rsqrt(jnp.mean(center * center, axis=-1, keepdims=True) + EPS)
    return center * inverse, inverse


def norm_back(grad, normed, inverse, gain):
    scaled = grad * gain
    back = inverse * (
        scaled
        - jnp.mean(scaled, axis=-1, keepdims=True)
        - normed * jnp.mean(scaled * normed, axis=-1, keepdims=True)
    )
    return back, jnp.sum(grad * normed, axis=0), jnp.sum(grad, axis=0)


def head_part(values, head):
    lane = lax.broadcasted_iota(jnp.int32, (1, LANES), 1)
    keep = (lane < HD) if head == 0 else (lane >= HD)
    return jnp.where(keep, values, jnp.zeros_like(values))


def lane_block(first):
    return pl.ds(pl.multiple_of(first, LANES), LANES)


def row_half(index, rows):
    return pl.ds(pl.multiple_of(index * rows, rows), rows)


def span(block, size=BLOCK):
    return slice(block * size, (block + 1) * size)


def vmem():
    return pl.BlockSpec(memory_space=pltpu.VMEM)


def smem():
    return pl.BlockSpec(memory_space=pltpu.SMEM)


def limit(mib):
    return pltpu.CompilerParams(vmem_limit_bytes=mib * 1024 * 1024)


def fill_halves(target, core, own, other):
    rows = own.shape[0]
    target[row_half(core, rows), :] = own[...]
    target[row_half(1 - core, rows), :] = other[...]


def split_halves(source, core, own, other):
    rows = own.shape[0]
    own[...] = source[row_half(core, rows), :]
    other[...] = source[row_half(1 - core, rows), :]


def attend_forward_kernel(info, qkv_own, qkv_other, out_own, out_other, qkv, out):
    length, core = info[0], info[1]
    blocks = qkv.shape[0] // BLOCK
    fill_halves(qkv, core, qkv_own, qkv_other)

    def part(block, which):
        return qkv[span(block), span(which, LANES)]

    column = lax.broadcasted_iota(jnp.int32, (1, BLOCK), 1)
    row = lax.broadcasted_iota(jnp.int32, (BLOCK, 1), 0)

    def score(block, head):
        query = head_part(part(block, 0), head) * jnp.asarray(0.125, BF16)
        last = jnp.minimum(row + block * BLOCK, length - 1)
        scores = []
        for other in range(block + 1):
            piece = dot(query, part(other, 1), NT)
            if other == block or (other + 1) * BLOCK > LEN_MIN:
                piece = jnp.where(column + other * BLOCK <= last, piece, MASKED)
            scores.append(piece)
        return scores

    tasks = [(block, head) for block in range(blocks) for head in range(2)]
    upcoming = score(*tasks[0])
    kept = None
    for place, (block, head) in enumerate(tasks):
        scores = upcoming
        if place + 1 < len(tasks):
            upcoming = score(*tasks[place + 1])
        top = functools.reduce(jnp.maximum, scores)
        top = jnp.max(top, axis=1, keepdims=True)
        weights = [jnp.exp(piece - top) for piece in scores]
        total = jnp.sum(functools.reduce(jnp.add, weights), axis=1, keepdims=True)
        mixed = functools.reduce(
            jnp.add,
            [
                dot(weight.astype(BF16), head_part(part(other, 2), head))
                for other, weight in enumerate(weights)
            ],
        )
        mixed = mixed / total
        if head == 0:
            kept = mixed
        else:
            out[span(block), :] = (kept + mixed).astype(BF16)
    split_halves(out, core, out_own, out_other)


def attend_forward(info, qkv_own, qkv_other):
    rows, width = qkv_own.shape[0], qkv_own.shape[1] // 3
    taken = pl.BlockSpec((rows, 3 * LANES), lambda pair: (0, pair))
    given = pl.BlockSpec((rows, LANES), lambda pair: (0, pair))
    shape = jax.ShapeDtypeStruct((rows, width), BF16)
    return pl.pallas_call(
        attend_forward_kernel,
        grid=(width // LANES,),
        in_specs=[smem(), taken, taken],
        out_specs=[given, given],
        out_shape=[shape, shape],
        scratch_shapes=[
            pltpu.VMEM((2 * rows, 3 * LANES), BF16),
            pltpu.VMEM((2 * rows, LANES), BF16),
        ],
        compiler_params=limit(32),
        name="attend_forward",
    )(info, qkv_own, qkv_other)


def attend_backward_kernel(
    info, qkv_own, qkv_other, grad_own, grad_other, back_own, back_other, qkv, grad, back, key_sum, value_sum
):
    length, core = info[0], info[1]
    blocks = qkv.shape[0] // BLOCK
    fill_halves(qkv, core, qkv_own, qkv_other)
    fill_halves(grad, core, grad_own, grad_other)
    key_sum[...] = jnp.zeros_like(key_sum)
    value_sum[...] = jnp.zeros_like(value_sum)
    eighth = jnp.asarray(0.125, BF16)

    def part(block, which):
        return qkv[span(block), span(which, LANES)]

    column = lax.broadcasted_iota(jnp.int32, (1, BLOCK), 1)
    row = lax.broadcasted_iota(jnp.int32, (BLOCK, 1), 0)

    def products(block, head):
        query = head_part(part(block, 0), head) * eighth
        mixed = head_part(grad[span(block), :], head)
        last = jnp.minimum(column + block * BLOCK, length - 1)
        scores, grads = [], []
        for other in range(block + 1):
            piece = dot(part(other, 1), query, NT)
            if other == block or (other + 1) * BLOCK > LEN_MIN:
                piece = jnp.where(row + other * BLOCK <= last, piece, MASKED)
            scores.append(piece)
            grads.append(dot(part(other, 2), mixed, NT))
        return query, mixed, scores, grads

    tasks = [(block, head) for block in range(blocks) for head in range(2)]
    upcoming = products(*tasks[0])
    kept = None
    for place, (block, head) in enumerate(tasks):
        query, mixed, scores, grads = upcoming
        if place + 1 < len(tasks):
            upcoming = products(*tasks[place + 1])
        top = jnp.max(functools.reduce(jnp.maximum, scores), axis=0, keepdims=True)
        weights = [jnp.exp(piece - top) for piece in scores]
        total = jnp.sum(functools.reduce(jnp.add, weights), axis=0, keepdims=True)
        inverse = 1.0 / total
        weights = [weight * inverse for weight in weights]
        products_sum = functools.reduce(jnp.add, [w * g for w, g in zip(weights, grads)])
        inner = jnp.sum(products_sum, axis=0, keepdims=True)
        query_sum = None
        for other in range(block + 1):
            weight = weights[other]
            change = (weight * (grads[other] - inner)).astype(BF16)
            value_sum[span(other), :] += dot(weight.astype(BF16), mixed)
            key_sum[span(other), :] += dot(change, query)
            piece = dot(change, head_part(part(other, 1), head) * eighth, TN)
            query_sum = piece if query_sum is None else query_sum + piece
        if head == 0:
            kept = query_sum
        else:
            back[span(block), span(0, LANES)] = (kept + query_sum).astype(BF16)
    back[:, span(1, LANES)] = key_sum[...].astype(BF16)
    back[:, span(2, LANES)] = value_sum[...].astype(BF16)
    split_halves(back, core, back_own, back_other)


def attend_backward(pair, info, qkv_own, qkv_other, grad_own, grad_other):
    rows = grad_own.shape[0]
    qkv_spec = pl.BlockSpec((rows, 3 * LANES), lambda step: (0, pair))
    grad_spec = pl.BlockSpec((rows, LANES), lambda step: (0, pair))
    shape = jax.ShapeDtypeStruct((rows, 3 * LANES), BF16)
    return pl.pallas_call(
        attend_backward_kernel,
        grid=(1,),
        in_specs=[smem(), qkv_spec, qkv_spec, grad_spec, grad_spec],
        out_specs=[vmem(), vmem()],
        out_shape=[shape, shape],
        scratch_shapes=[
            pltpu.VMEM((2 * rows, 3 * LANES), BF16),
            pltpu.VMEM((2 * rows, LANES), BF16),
            pltpu.VMEM((2 * rows, 3 * LANES), BF16),
            pltpu.VMEM((2 * rows, LANES), F32),
            pltpu.VMEM((2 * rows, LANES), F32),
        ],
        compiler_params=limit(32),
        name=f"attend_backward_{pair}",
    )(info, qkv_own, qkv_other, grad_own, grad_other)


def feed_kernel(two, grad, weight, bias, active, grad_pre, mlp, back, bias_sum):
    hidden = active.shape[1]
    slope = math.sqrt(2.0 / math.pi)
    cubic = slope * 0.044715
    for chunk in range(hidden // BLOCK):
        here = span(chunk)
        there = slice(hidden + chunk * BLOCK, hidden + (chunk + 1) * BLOCK)
        pre = dot(two[...], weight[:, here]) + bias[:, here]
        grad_active = dot(grad[...], weight[:, there])
        square = pre * pre
        half = 0.5 + 0.5 * jnp.tanh(pre * (slope + cubic * square))
        value = pre * half
        change = half + (value - value * half) * (2.0 * slope + (6.0 * cubic) * square)
        active[:, here] = value.astype(BF16)
        low = (grad_active * change).astype(BF16)
        grad_pre[:, here] = low
        bias_sum[:, here] = jnp.sum(low.astype(F32), axis=0, keepdims=True)
    for chunk in range(mlp.shape[1] // BLOCK):
        here = span(chunk)
        back[:, here] = dot(grad_pre[...], weight[here, :hidden], NT).astype(back.dtype)
        mlp[:, here] = dot(active[...], weight[here, hidden:], NT).astype(mlp.dtype)


def feed(two, grad, weight, bias, result, name):
    rows, width = two.shape
    hidden = weight.shape[1] // 2
    low = jax.ShapeDtypeStruct((rows, hidden), BF16)
    terms = jax.ShapeDtypeStruct((rows, width), result)
    return pl.pallas_call(
        feed_kernel,
        in_specs=[vmem()] * 4,
        out_specs=[vmem()] * 5,
        out_shape=[low, low, terms, terms, jax.ShapeDtypeStruct((1, hidden), F32)],
        compiler_params=limit(24),
        name=name,
    )(two, grad, weight, bias)


def weight_grads_kernel(count, shard, order, *refs):
    lefts_own, lefts_other = refs[:count], refs[count : 2 * count]
    rights_own, rights_other = refs[2 * count : 3 * count], refs[3 * count : 4 * count]
    out, total = refs[4 * count], refs[4 * count + 1]
    first = 0
    for term in range(count):
        columns = rights_own[term].shape[1]
        for chunk in range(total.shape[0] // BLOCK):
            here = span(chunk)
            piece = dot(lefts_own[term][:, here], rights_own[term][...], TN)
            piece += dot(lefts_other[term][:, here], rights_other[term][...], TN)
            total[here, first : first + columns] = piece.astype(BF16)
        first += columns
    for place in range(total.shape[0] // shard):
        start = pl.multiple_of(order[place] * shard, 16)
        out[span(place, shard), :] = total[pl.ds(start, shard), :]


def weight_grads(order, terms, name):
    width = terms[0][0].shape[1]
    columns = sum(term[2].shape[1] for term in terms)
    shard = width // order.shape[0]
    operands = [term[kind] for kind in range(4) for term in terms]
    return pl.pallas_call(
        functools.partial(weight_grads_kernel, len(terms), shard),
        in_specs=[smem()] + [vmem()] * len(operands),
        out_specs=vmem(),
        out_shape=jax.ShapeDtypeStruct((width, columns), BF16),
        scratch_shapes=[pltpu.VMEM((width, columns), BF16)],
        compiler_params=limit(24),
        name=name,
    )(order, *operands)


def place_kernel(shard, order, *refs):
    pieces, out = refs[:-1], refs[-1]
    place = 0
    for piece in pieces:
        for step in range(piece.shape[0] // shard):
            start = pl.multiple_of(order[place] * shard, 16)
            out[pl.ds(start, shard), :] = piece[span(step, shard), :]
            place += 1


def place_blocks(order, pieces):
    shard, columns = pieces[0].shape
    return pl.pallas_call(
        functools.partial(place_kernel, shard),
        in_specs=[smem()] + [vmem()] * len(pieces),
        out_specs=vmem(),
        out_shape=jax.ShapeDtypeStruct((shard * order.shape[0], columns), BF16),
        name="place_blocks",
    )(order, *pieces)


class Cube:
    def __init__(self, shard_rows):
        self.shard_rows = shard_rows
        self.zy = lax.axis_size("zy")
        self.cores = lax.axis_size("core")
        self.size = self.zy * lax.axis_size("x")
        self.bits = self.size.bit_length() - 1
        self.direct = self.size == 1 << self.bits and self.bits >= 2 and shard_rows % 16 == 0
        outer = list(range(self.bits - 1, 1, -1))
        self.dims = [outer + [0, 1], outer + [1, 0]]
        if self.direct:
            masks = [
                [sum(1 << dims[step] for step in range(self.bits) if place >> step & 1) for place in range(self.size)]
                for dims in self.dims
            ]
            mine = lax.axis_index("zy") * 2 + lax.axis_index("x")
            core = lax.axis_index("core")
            chosen = jnp.where(core == 0, jnp.array(masks[0], jnp.int32), jnp.array(masks[1], jnp.int32))
            self.order = jnp.bitwise_xor(mine.astype(jnp.int32), chosen)
        else:
            blocks = shard_rows * self.size // 48
            self.order = jnp.arange(blocks, dtype=jnp.int32)

    def send(self, values, step):
        pairs = []
        for zy in range(self.zy):
            for core in range(self.cores):
                for x in range(2):
                    other = (zy * 2 + x) ^ (1 << self.dims[core][step])
                    pairs.append(((zy * 2 + core) * 2 + x, (other // 2 * 2 + core) * 2 + other % 2))
        return lax.ppermute(values, ("zy", "core", "x"), pairs)

    def gather(self, shard):
        if not self.direct:
            return lax.all_gather(shard, ("zy", "x"), axis=0, tiled=True)
        pieces = [shard]
        for step in range(self.bits):
            payload = pieces[0] if step == 0 else jnp.concatenate(pieces, axis=0)
            pieces.append(self.send(payload, step))
        return place_blocks(self.order, pieces)

    def steps(self):
        return self.bits if self.direct else 1

    def reduce_step(self, values, step):
        if not self.direct:
            return lax.psum_scatter(values, ("zy", "x"), scatter_dimension=0, tiled=True)
        half = values.shape[0] // 2
        received = self.send(values[half:], self.bits - 1 - step)
        return (values[:half].astype(F32) + received.astype(F32)).astype(BF16)


def swap_small(values):
    return lax.ppermute(values, ("core", "x"), [(0, 0), (1, 2), (2, 1), (3, 3)])


def swap(values):
    received = lax.ppermute(values, ("core", "x"), [(1, 2), (2, 1)])
    return jnp.where(lax.axis_index("core") == lax.axis_index("x"), values, received)


def exchange(values):
    return lax.ppermute(values, "core", [(0, 1), (1, 0)])


def tie(values, other):
    return lax.optimization_barrier((values, other))


def shards(
    hidden_in,
    seq_lens,
    ln1_gain,
    ln1_bias,
    w_qkv,
    bias_qv,
    w_out,
    bias_out,
    ln2_gain,
    ln2_bias,
    w_up,
    bias_up,
    w_down,
    bias_down,
    grad_out,
):
    core = lax.axis_index("core")
    group = ("zy", "x")
    everyone = ("zy", "core", "x")
    rows, width = hidden_in.shape
    shard_rows = w_up.shape[0]
    head_cols = w_qkv.shape[2]
    hidden_cols = w_up.shape[1]
    pairs = head_cols // LANES
    qkv_cols = 3 * head_cols
    cube = Cube(shard_rows)

    qkv_shard = w_qkv.reshape(3, shard_rows, pairs, LANES).transpose(1, 2, 0, 3).reshape(shard_rows, qkv_cols)
    attn_shard = swap_small(jnp.concatenate([qkv_shard, w_out.T], axis=1))
    length = swap_small(seq_lens)[0]
    residual_low = swap(hidden_in)
    mlp_shard = swap_small(jnp.concatenate([w_up, w_down.T], axis=1))
    attn_weights = cube.gather(attn_shard)
    mlp_weights = lax.all_gather(mlp_shard, group, axis=0, tiled=True)
    grad_low = swap(grad_out)

    qkv_weight, out_weight = attn_weights[:, :qkv_cols], attn_weights[:, qkv_cols:]
    info = jnp.stack([length, core.astype(jnp.int32)])

    residual = residual_low.astype(F32)
    unit_one, inverse_one = norm_stats(residual)
    norm_own = (unit_one * ln1_gain + ln1_bias).astype(BF16)
    norm_other = exchange(norm_own)
    bias_here = lax.dynamic_slice_in_dim(bias_qv, core * head_cols, head_cols, 1)
    qkv_bias = jnp.stack([bias_here[0], jnp.zeros((head_cols,), F32), bias_here[1]])
    qkv_bias = qkv_bias.reshape(3, pairs, LANES).transpose(1, 0, 2).reshape(qkv_cols)
    qkv_own = (dot(norm_own, qkv_weight) + qkv_bias).astype(BF16)
    qkv_other = (dot(norm_other, qkv_weight) + qkv_bias).astype(BF16)
    mixed_own, mixed_other = attend_forward(info, qkv_own, qkv_other)
    attn_received = exchange(dot(mixed_other, out_weight, NT).astype(BF16))
    hidden = residual + (dot(mixed_own, out_weight, NT) + attn_received.astype(F32)) + bias_out
    unit_two, inverse_two = norm_stats(hidden)
    two_own = (unit_two * ln2_gain + ln2_bias).astype(BF16)
    two_other = exchange(two_own)
    bias_up_here = lax.dynamic_slice_in_dim(bias_up, core * hidden_cols, hidden_cols, 0)[None]

    slots = core * rows + jnp.arange(rows, dtype=jnp.int32)
    grad_own = jnp.where((slots < length)[:, None], grad_low, jnp.zeros_like(grad_low))
    grad_other = exchange(grad_own)

    active_other, grad_pre_other, mlp_other, back_two_other, up_sum_other = feed(
        two_other, grad_other, mlp_weights, bias_up_here, BF16, "feed_other"
    )
    back_two_received = exchange(back_two_other)
    mlp_received = exchange(mlp_other)
    active_own, grad_pre_own, mlp_own, back_two_own, up_sum_own = feed(
        two_own, grad_own, mlp_weights, bias_up_here, F32, "feed_own"
    )
    layer_out = swap((hidden + (mlp_own + mlp_received.astype(F32)) + bias_down).astype(BF16))

    back_two = back_two_own + back_two_received.astype(F32)
    back_hidden, gain_two_sum, shift_two_sum = norm_back(back_two, unit_two, inverse_two, ln2_gain)
    grad_hidden = grad_own.astype(F32) + back_hidden
    attn_grad_own = grad_hidden.astype(BF16)
    attn_grad_other = exchange(attn_grad_own)
    first_grads = weight_grads(
        cube.order,
        [
            (two_own, two_other, grad_pre_own, grad_pre_other),
            (grad_own, grad_other, active_own, active_other),
            (attn_grad_own, attn_grad_other, mixed_own, mixed_other),
        ],
        "first_weight_grads",
    )
    grad_mixed_own = dot(attn_grad_own, out_weight).astype(BF16)
    grad_mixed_other = dot(attn_grad_other, out_weight).astype(BF16)

    def place(values, full):
        return lax.dynamic_update_slice_in_dim(
            jnp.zeros(values.shape[:-1] + (full,), F32), values, core * values.shape[-1], values.ndim - 1
        )

    early = jnp.concatenate(
        [
            jnp.sum(grad_own.astype(F32), axis=0),
            gain_two_sum,
            shift_two_sum,
            jnp.sum(attn_grad_own.astype(F32), axis=0),
            place((up_sum_own + up_sum_other)[0], bias_up.shape[0]),
        ]
    )
    early = jnp.sum(lax.all_gather(early, everyone), axis=0)

    backs_own, backs_other = [], []
    grad_pair = (grad_mixed_own, grad_mixed_other)
    for pair in range(pairs):
        if pair < cube.steps():
            first_grads, grad_pair = tie(first_grads, grad_pair)
            first_grads = cube.reduce_step(first_grads, pair)
        back_own, back_other = attend_backward(pair, info, qkv_own, qkv_other, *grad_pair)
        backs_own.append(back_own)
        backs_other.append(back_other)
    for step in range(pairs, cube.steps()):
        first_grads = cube.reduce_step(first_grads, step)
    back_own = jnp.concatenate(backs_own, axis=1)
    back_other = jnp.concatenate(backs_other, axis=1)

    last_grads = weight_grads(
        cube.order, [(norm_own, norm_other, back_own, back_other)], "last_weight_grads"
    )
    for step in range(cube.steps()):
        last_grads = cube.reduce_step(last_grads, step)
    back_one_received = exchange(dot(back_other, qkv_weight, NT).astype(BF16))
    back_one = dot(back_own, qkv_weight, NT) + back_one_received.astype(F32)
    back_input, gain_one_sum, shift_one_sum = norm_back(back_one, unit_one, inverse_one, ln1_gain)
    grad_input = swap((grad_hidden + back_input).astype(BF16)).astype(F32)

    back_sum = jnp.sum(back_own.astype(F32), axis=0) + jnp.sum(back_other.astype(F32), axis=0)
    back_sum = back_sum.reshape(pairs, 3, LANES).transpose(1, 0, 2).reshape(3, head_cols)
    qv_sum = jnp.stack([back_sum[0], back_sum[2]])
    late = jnp.concatenate([gain_one_sum, shift_one_sum, place(qv_sum, width).reshape(-1)])
    late = jnp.sum(lax.all_gather(late, everyone), axis=0)
    down_bias, gain_two, shift_two, out_bias, up_bias = jnp.split(early, [width * n for n in range(1, 5)])
    gain_one, shift_one, qv_bias = jnp.split(late, [width, 2 * width])

    first_grads = swap_small(first_grads)
    last_grads = swap_small(last_grads)
    grad_w_qkv = last_grads.reshape(shard_rows, pairs, 3, LANES).transpose(2, 0, 1, 3)
    grad_w_qkv = grad_w_qkv.reshape(3, shard_rows, head_cols).astype(F32)
    grad_w_up = first_grads[:, :hidden_cols].astype(F32)
    grad_w_down = first_grads[:, hidden_cols : 2 * hidden_cols].T.astype(F32)
    grad_w_out = first_grads[:, 2 * hidden_cols :].T.astype(F32)
    return (
        layer_out,
        grad_input,
        gain_one,
        shift_one,
        grad_w_qkv,
        qv_bias.reshape(2, width),
        grad_w_out,
        out_bias,
        gain_two,
        shift_two,
        grad_w_up,
        up_bias,
        grad_w_down,
        down_bias,
    )


def solution(mesh):
    cores = 2
    devices = mesh.devices
    inner = Mesh(devices.reshape(devices.shape[0] // cores, cores, devices.shape[1]), ("zy", "core", "x"))
    dp = ("zy", "core")
    token = P(("zy", "core", "x"), None)
    in_specs = (
        token,
        P(dp),
        P(),
        P(),
        P(None, dp, "x"),
        P(),
        P("x", dp),
        P(),
        P(),
        P(),
        P(dp, "x"),
        P(),
        P("x", dp),
        P(),
        token,
    )
    out_specs = (
        token,
        token,
        P(),
        P(),
        P(None, dp, "x"),
        P(),
        P("x", dp),
        P(),
        P(),
        P(),
        P(dp, "x"),
        P(),
        P("x", dp),
        P(),
    )
    return jax.shard_map(shards, mesh=inner, in_specs=in_specs, out_specs=out_specs, check_vma=False)
```

time: 559 us -> 563 us (level)
  waiting for transfers between devices: 248 us -> 105 us
  blocking collectives: 48.4 us -> 145 us
  matrix products: 82.4 us -> 21.3 us
  Pallas kernels: 64.5 us -> 97.1 us
  starting transfers between devices: 46.5 us -> 76.7 us
  local copies, waits for them, and re-layouts: 18.6 us -> 45.9 us
  other arithmetic: 24 us -> 47.2 us
    reduce_scatter x2 -> x0, waiting for transfers between devices: 150 us -> none  [the longest x1 134 us: shards(): lax.psum_scatter(mlp_grads, group, scatter_dimension=0, tiled=True)]
    all_gather x0 -> x2, blocking collectives: none -> 145 us  [the longest x1 73.5 us: shards(): early = jnp.sum(lax.all_gather(early, everyone), axis=0)]
    ppermute x9 -> x21, waiting for transfers between devices: 38.9 us -> 102 us  [the longest x12 81.6 us: send(): return lax.ppermute(values, ('zy', 'core', 'x'), pairs)]
    dot_general x24 -> x8, matrix products: 82.4 us -> 21.3 us  [dot(): return lax.dot_general(left, right, dims, preferred_element_type=F32)]
    psum x1 -> x0, blocking collectives: 48.4 us -> none  [shards(): late = lax.psum(late, everyone)]
    pallas_call x2 -> x9, Pallas kernels: 64.5 us -> 97.1 us  [the longest x3 39.3 us: attend_backward(): pl.pallas_call(attend_backward_kernel, grid=(1,), in_specs=[smem(), qkv_s...]
    all_gather x1, waiting for transfers between devices: 30.5 us -> 0.01 us  [shards(): mlp_weights = lax.all_gather(mlp_shard, group, axis=0, tiled=True)]
    all_gather x1 -> x0, waiting for transfers between devices: 27.2 us -> none  [shards(): attn_weights = lax.all_gather(attn_shard, group, axis=0, tiled=True)]
  transfers between devices with their start and end apart: 21 -> 30, of which waited for: 12 -> 14; matrix products, arithmetic and copies ran while one was open for 17% -> 15% of each run, Pallas kernels for 3% -> 13%
where the time goes in v2:
time: 563 us; the launch traced here: 553 us
  blocking collectives  145 us (26%)
  waiting for transfers between devices  105 us (19%)
  Pallas kernels  97.1 us (17%)
  starting transfers between devices  76.7 us (14%)
  other arithmetic  47.2 us (8%)
  local copies, waits for them, and re-layouts  45.9 us (8%)
  matrix products  21.3 us (4%)
  between operations  15.3 us (3%)
    ppermute x12, waiting for transfers between devices, send(): return lax.ppermute(values, ('zy', 'core', 'x'), pairs)  81.6 us
    all_gather x1, blocking collectives, shards(): early = jnp.sum(lax.all_gather(early, everyone), axis=0)  73.5 us
    all_gather x1, blocking collectives, shards(): late = jnp.sum(lax.all_gather(late, everyone), axis=0)  71.4 us
    pallas_call x3, Pallas kernels, attend_backward(): pl.pallas_call(attend_backward_kernel, grid=(1,), in_specs=[smem(), qkv_s...  39.3 us
    ppermute x8, starting transfers between devices, exchange(): return lax.ppermute(values, 'core', [(0, 1), (1, 0)])  36.7 us
    pallas_call x2, Pallas kernels, feed(): pl.pallas_call(feed_kernel, in_specs=[vmem()] * 4, out_specs=[vmem()] * 5...  23.6 us
    unnamed x133, local copies, waits for them, and re-layouts  23.5 us
    dot_general x8, matrix products, dot(): return lax.dot_general(left, right, dims, preferred_element_type=F32)  21.3 us
  transfers between devices with their start and end apart: 30, of which 14 were waited for; matrix products, arithmetic and copies ran while one was open for 15% of the time, Pallas kernels for 13%

profile of v2, /device:TPU:1, one launch (start us, length us, event | category | flops | bytes accessed | tf_op | source)
XLA Modules:
  0.0 553.1 jit_solution(12927816556914843698)
XLA Ops:
  8.3 4.5 collective-permute-start.10
  14.0 3.2 collective-permute-done.10
  18.8 3.6 collective-permute-start.2
  22.4 3.1 collective-permute-done.2.refs_0_
  25.5 2.3 collective-permute-start.3
  27.8 4.9 collective-permute-done.3.refs_1_
  32.7 3.1 collective-permute-start.4
  35.8 5.4 collective-permute-start
  44.6 12.3 %collective-permute-done.5.refs_3_ = bf16[192,1536]{1,0:T(8,128)(2,1)S(1)} collective-permute-done((bf16[192,1536]{1,0:T(8,128)(2,1)}, bf16[192,1536]{1,0:T(8,128)(2,1)S(1)}, u32[]{:S(2)}, u32[]{:S(2)}) %collective-permute-start.5) | collective-permute-done | bytes 589856 | tf_op jit(solution)/shard_map/ppermute | solution.py:361
  58.2 11.0 %collective-permute-done = bf16[768,768]{1,0:T(8,128)(2,1)S(1)} collective-permute-done((bf16[768,768]{1,0:T(8,128)(2,1)S(1)}, bf16[768,768]{1,0:T(8,128)(2,1)S(1)}, u32[]{:S(2)}, u32[]{:S(2)}) %collective-permute-start) | collective-permute-done | bytes 1179680 | tf_op jit(solution)/shard_map/ppermute | solution.py:388
  71.2 12.1 %collective-permute-start.7 = (bf16[768,768]{1,0:T(8,128)(2,1)S(1)}, bf16[768,768]{1,0:T(8,128)(2,1)}, u32[]{:S(2)}, u32[]{:S(2)}) collective-permute-start(bf16[768,768]{1,0:T(8,128)(2,1)S(1)} %fusion.9.refs_0_), channel_id=1, source_target_pairs={{0,2},{2,0},{1,3},{3,1},{4,6},{6,4},{5,7},{7,5},{8,10},{10,8},{9,1... | collective-permute-start | bytes 3538952 | tf_op jit(solution)/shard_map/ppermute | solution.py:393
  83.3 1.9 collective-permute-start.1
  85.2 3.6 collective-permute-start.9
  90.4 3.2 place_blocks.1
  93.7 3.3 fusion.qkv_own
  97.0 3.0 fusion.1.qkv_other
  100.0 14.9 %attend_forward.1 = (bf16[768,384]{1,0:T(8,128)(2,1)S(1)}, bf16[768,384]{1,0:T(8,128)(2,1)S(1)}) custom-call(s32[2]{0:T(128)S(1)} %pad_add_fusion.info, bf16[768,1152]{1,0:T(8,128)(2,1)S(1)} %fusion.qkv_own, bf16[768,1152]{1,0:T(8,128)(2,1)S(1)} %fusion.1.qkv_other), custom_call_target="tpu_custom_call" | custom-call | tf_op jit(solution)/shard_map/attend_forward/pallas_call | solution.py:139
  115.7 1.8 convolution_convert_fusion.1
  118.4 20.9 %collective-permute-start.8 = (bf16[768,768]{1,0:T(8,128)(2,1)}, bf16[768,768]{1,0:T(8,128)(2,1)}, u32[]{:S(2)}, u32[]{:S(2)}) collective-permute-start(bf16[768,768]{1,0:T(8,128)(2,1)} %convolution_convert_fusion.1), channel_id=1, source_target_pairs={{0,2},{2,0},{1,3},{3,1},{4,6},{6,4},{5,7},{7,5},{8,10},{10,8},{9,1... | collective-permute-start | bytes 3538952 | tf_op jit(solution)/shard_map/ppermute | solution.py:393
  140.2 3.3 convert_reduce_fusion.3
  143.5 2.5 fusion.30
  146.8 1.5 add_convert_fusion.3.two.refs_0_
  149.5 2.0 collective-permute-done.11.two.refs_3_
  151.6 2.3 copy-done.1
  153.9 12.2 %feed_other.1 = (bf16[768,1536]{1,0:T(8,128)(2,1)S(1)}, bf16[768,1536]{1,0:T(8,128)(2,1)S(1)}, bf16[768,768]{1,0:T(8,128)(2,1)}, bf16[768,768]{1,0:T(8,128)(2,1)}, f32[1,1536]{1,0:T(1,128)S(1)}) custom-call(bf16[768,768]{1,0:T(8,128)(2,1)} %collective-permute-done.11.two.refs_3_, bf16[768,768]{1,0:T(8,128)(2,1)} %collective-permute-done.12.grad.refs_4_, ...), custom_call_target="tpu_custom_call" | custom-call | tf_op jit(solution)/shard_map/feed_other/pallas_call | solution.py:266
  166.1 1.5 copy-done.10
  171.4 2.3 copy-done.2
  173.7 11.4 %feed_own.1 = (bf16[768,1536]{1,0:T(8,128)(2,1)S(1)}, bf16[768,1536]{1,0:T(8,128)(2,1)S(1)}, f32[768,768]{1,0:T(8,128)S(1)}, f32[768,768]{1,0:T(8,128)S(1)}, f32[1,1536]{1,0:T(1,128)S(1)}) custom-call(bf16[768,768]{1,0:T(8,128)(2,1)} %add_convert_fusion.3.two.refs_0_, bf16[768,768]{1,0:T(8,128)(2,1)} %get-tuple-element.80.grad.refs_1_, ...), custom_call_target="tpu_custom_call" | custom-call | tf_op jit(solution)/shard_map/feed_own/pallas_call | solution.py:266
  185.1 3.1 multiply_reduce_fusion
  189.6 5.2 convert_reduce_fusion.4
  195.3 1.6 convolution_convert_fusion.3.grad_own
  197.7 1.6 convolution_convert_fusion.2.grad_other
  199.4 11.4 %first_weight_grads.1 = bf16[768,3456]{1,0:T(8,128)(2,1)S(1)} custom-call(s32[16]{0:T(128)S(1)} %copy-done.19, bf16[768,768]{1,0:T(8,128)(2,1)} %add_convert_fusion.3.two.refs_0_, bf16[768,768]{1,0:T(8,128)(2,1)} %get-tuple-element.80.grad.refs_1_, bf16[768,768]{1,0:T(8,128)(2,1)S(1)} %get-tuple-element.77.refs_2_, ...), custom_call_target="tpu_custom_call" | custom-call | tf_op jit(solution)/shard_map/first_weight_grads/pallas_call | solution.py:299
  210.9 1.9 slice.94
  217.2 2.9 collective-permute-start.14
  224.0 36.2 %collective-permute-done.17 = bf16[384,3456]{1,0:T(8,128)(2,1)} collective-permute-done((bf16[384,3456]{1,0:T(8,128)(2,1)}, bf16[384,3456]{1,0:T(8,128)(2,1)}, u32[]{:S(2)}, u32[]{:S(2)}) %collective-permute-start.17) | collective-permute-done | bytes 2654240 | tf_op jit(solution)/shard_map/ppermute | solution.py:361
  260.3 3.2 add_convert_fusion
  263.4 1.5 copy-done.27
  266.1 73.5 %all-gather.1 = f32[196608]{0:T(1024)} all-gather(f32[6144]{0:T(1024)S(1)} %copy-done.53), channel_id=3, replica_groups=mesh['zy'=8,'core'=2,'x'=2] {'zy','core','x'}, dimensions={0}, use_global_device_ids=true | all-gather | bytes 811008 | tf_op jit(solution)/shard_map/all_gather | solution.py:502
  339.7 2.1 reshape.121
  341.8 1.8 reduce_sum.179
  348.4 13.3 %attend_backward_0.1 = (bf16[768,384]{1,0:T(8,128)(2,1)S(1)}, bf16[768,384]{1,0:T(8,128)(2,1)S(1)}) custom-call(s32[2]{0:T(128)S(1)} %pad_add_fusion.info, bf16[768,1152]{1,0:T(8,128)(2,1)S(1)} %fusion.qkv_own, bf16[768,1152]{1,0:T(8,128)(2,1)S(1)} %fusion.1.qkv_other, bf16[768,384]{1,0:T(8,128)(2,1)S(1)} %copy-done.6, bf16[768,384]{1,0:T(8,128)(2,1)S(1)} %copy-done.7), custom_call_target="tpu_custom_call" | custom-call | tf_op jit(solution)/shard_map/attend_backward_0/pallas_call | solution.py:220
  363.0 2.4 broadcast_select_fusion
  365.4 13.0 %attend_backward_1.1 = (bf16[768,384]{1,0:T(8,128)(2,1)S(1)}, bf16[768,384]{1,0:T(8,128)(2,1)S(1)}) custom-call(s32[2]{0:T(128)S(1)} %pad_add_fusion.info, bf16[768,1152]{1,0:T(8,128)(2,1)S(1)} %fusion.qkv_own, bf16[768,1152]{1,0:T(8,128)(2,1)S(1)} %fusion.1.qkv_other, bf16[768,384]{1,0:T(8,128)(2,1)S(1)} %copy-done.6, bf16[768,384]{1,0:T(8,128)(2,1)S(1)} %copy-done.7), custom_call_target="tpu_custom_call" | custom-call | tf_op jit(solution)/shard_map/attend_backward_1/pallas_call | solution.py:220
  378.7 1.6 add_convert_fusion.1
  381.7 13.0 %attend_backward_2.1 = (bf16[768,384]{1,0:T(8,128)(2,1)S(1)}, bf16[768,384]{1,0:T(8,128)(2,1)S(1)}) custom-call(s32[2]{0:T(128)S(1)} %pad_add_fusion.info, bf16[768,1152]{1,0:T(8,128)(2,1)S(1)} %fusion.qkv_own, bf16[768,1152]{1,0:T(8,128)(2,1)S(1)} %fusion.1.qkv_other, bf16[768,384]{1,0:T(8,128)(2,1)S(1)} %copy-done.6, bf16[768,384]{1,0:T(8,128)(2,1)S(1)} %copy-done.7), custom_call_target="tpu_custom_call" | custom-call | tf_op jit(solution)/shard_map/attend_backward_2/pallas_call | solution.py:220
  397.0 4.7 last_weight_grads.1
  403.3 3.8 convolution_convert_fusion
  407.2 2.2 collective-permute-start.19
  409.4 1.4 add_convert_fusion.5
  411.0 4.2 collective-permute-done.21
  417.4 10.9 %collective-permute-done.27 = bf16[48,3456]{1,0:T(8,128)(2,1)S(1)} collective-permute-done((bf16[48,3456]{1,0:T(8,128)(2,1)S(1)}, bf16[48,3456]{1,0:T(8,128)(2,1)S(1)}, u32[]{:S(2)}, u32[]{:S(2)}) %collective-permute-start.27) | collective-permute-done | bytes 331808 | tf_op jit(solution)/shard_map/ppermute | solution.py:361
  429.2 2.9 collective-permute-start.28
  432.2 3.6 fusion.15
  437.0 71.4 %all-gather = f32[98304]{0:T(1024)} all-gather(f32[3072]{0:T(1024)S(1)} %pad_maximum_fusion.5), channel_id=2, replica_groups=mesh['zy'=8,'core'=2,'x'=2] {'zy','core','x'}, dimensions={0}, use_global_device_ids=true | all-gather | bytes 405504 | tf_op jit(solution)/shard_map/all_gather | solution.py:532
  508.4 1.8 reshape.120
  513.2 3.2 fusion.14
  516.4 5.1 collective-permute-start.20
  523.4 6.0 %collective-permute-done.23 = bf16[96,1152]{1,0:T(8,128)(2,1)S(1)} collective-permute-done((bf16[96,1152]{1,0:T(8,128)(2,1)S(1)}, bf16[96,1152]{1,0:T(8,128)(2,1)S(1)}, u32[]{:S(2)}, u32[]{:S(2)}) %collective-permute-start.23) | collective-permute-done | bytes 221216 | tf_op jit(solution)/shard_map/ppermute | solution.py:361
  529.6 1.8 convert_bitcast_fusion
  531.4 5.9 %collective-permute-done.24 = bf16[48,1152]{1,0:T(8,128)(2,1)S(1)} collective-permute-done((bf16[48,1152]{1,0:T(8,128)(2,1)S(1)}, bf16[48,1152]{1,0:T(8,128)(2,1)S(1)}, u32[]{:S(2)}, u32[]{:S(2)}) %collective-permute-start.24) | collective-permute-done | bytes 110624 | tf_op jit(solution)/shard_map/ppermute | solution.py:361
  537.3 1.9 collective-permute-start.25
  540.6 2.7 collective-permute-done.25
  544.4 1.6 select_convert_fusion
  (231 shorter events, 55.6 us)
Async XLA Ops:
  7.2 28.7 %copy-start.42 = (bf16[768,768]{1,0:T(8,128)(2,1)S(1)}, bf16[768,768]{1,0:T(8,128)(2,1)}, u32[]{:S(2)}) copy-start(bf16[768,768]{1,0:T(8,128)(2,1)} %param.17) | copy-start | bytes 3538948
  7.2 144.4 %all-gather.4.cloned.1.call-start = ((), (), s32[]{:S(2)}) async-start(), calls=%async_computation | async-start | bytes 5013504 | tf_op jit(solution)/shard_map/all_gather | solution.py:434
  8.3 8.9 %collective-permute-start.10 = (bf16[48,3072]{1,0:T(8,128)(2,1)S(1)}, bf16[48,3072]{1,0:T(8,128)(2,1)S(1)}, u32[]{:S(2)}, u32[]{:S(2)}) collective-permute-start(bf16[48,3072]{1,0:T(8,128)(2,1)S(1)} %pad_maximum_fusion.3), channel_id=1, source_target_pairs={{0,0},{1,2},{2,1},{3,3},{4,4},{5,6},{6,5},{7,7},{8,8},{9,10},{10,9... | collective-permute-start | bytes 884744 | tf_op jit(solution)/shard_map/ppermute | solution.py:384
  18.8 6.8 %collective-permute-start.2 = (bf16[48,1536]{1,0:T(8,128)(2,1)S(1)}, bf16[48,1536]{1,0:T(8,128)(2,1)S(1)}, u32[]{:S(2)}, u32[]{:S(2)}) collective-permute-start(bf16[48,1536]{1,0:T(8,128)(2,1)S(1)} %pad_maximum_fusion.4), channel_id=1, source_target_pairs={{0,0},{1,2},{2,1},{3,3},{4,4},{5,6},{6,5},{7,7},{8,8},{9,10},{10,9... | collective-permute-start | bytes 442376 | tf_op jit(solution)/shard_map/ppermute | solution.py:384
  25.5 44.1 %copy-start.39 = (bf16[48,1536]{1,0:T(8,128)(2,1)}, bf16[48,1536]{1,0:T(8,128)(2,1)S(1)}, u32[]{:S(2)}) copy-start(bf16[48,1536]{1,0:T(8,128)(2,1)S(1)} %collective-permute-done.2.refs_0_) | copy-start | bytes 442372
  25.5 7.2 %collective-permute-start.3 = (bf16[48,1536]{1,0:T(8,128)(2,1)S(1)}, bf16[48,1536]{1,0:T(8,128)(2,1)S(1)}, u32[]{:S(2)}, u32[]{:S(2)}) collective-permute-start(bf16[48,1536]{1,0:T(8,128)(2,1)S(1)} %collective-permute-done.2.refs_0_), channel_id=1, source_target_pairs={{0,16},{1,17},{2,18},{3,19},{4,20},{5,21},{6,22},{7,23},{8,24},{9,... | collective-permute-start | bytes 442376 | tf_op jit(solution)/shard_map/ppermute | solution.py:361
  32.7 36.9 %copy-start.40 = (bf16[48,1536]{1,0:T(8,128)(2,1)}, bf16[48,1536]{1,0:T(8,128)(2,1)S(1)}, u32[]{:S(2)}) copy-start(bf16[48,1536]{1,0:T(8,128)(2,1)S(1)} %collective-permute-done.3.refs_1_) | copy-start | bytes 442372
  32.7 9.7 %collective-permute-start.4 = (bf16[96,1536]{1,0:T(8,128)(2,1)S(1)}, bf16[96,1536]{1,0:T(8,128)(2,1)S(1)}, u32[]{:S(2)}, u32[]{:S(2)}) collective-permute-start(bf16[96,1536]{1,0:T(8,128)(2,1)S(1)} %pad_maximum_fusion.2), channel_id=1, source_target_pairs={{0,8},{1,9},{2,10},{3,11},{4,12},{5,13},{6,14},{7,15},{8,0},{9,1},... | collective-permute-start | bytes 884744 | tf_op jit(solution)/shard_map/ppermute | solution.py:361
  35.8 33.4 %collective-permute-start = (bf16[768,768]{1,0:T(8,128)(2,1)S(1)}, bf16[768,768]{1,0:T(8,128)(2,1)S(1)}, u32[]{:S(2)}, u32[]{:S(2)}) collective-permute-start(bf16[768,768]{1,0:T(8,128)(2,1)S(1)} %copy-done.42), channel_id=1, source_target_pairs={{1,2},{2,1},{5,6},{6,5},{9,10},{10,9},{13,14},{14,13},{17,18},{18,... | collective-permute-start | bytes 3538952 | tf_op jit(solution)/shard_map/ppermute | solution.py:388
  42.5 27.2 %copy-start.38 = (bf16[96,1536]{1,0:T(8,128)(2,1)}, bf16[96,1536]{1,0:T(8,128)(2,1)S(1)}, u32[]{:S(2)}) copy-start(bf16[96,1536]{1,0:T(8,128)(2,1)S(1)} %collective-permute-done.4.refs_2_) | copy-start | bytes 884740
  43.4 13.6 %collective-permute-start.5 = (bf16[192,1536]{1,0:T(8,128)(2,1)}, bf16[192,1536]{1,0:T(8,128)(2,1)S(1)}, u32[]{:S(2)}, u32[]{:S(2)}) collective-permute-start(bf16[192,1536]{1,0:T(8,128)(2,1)} %pad_maximum_fusion.1), channel_id=1, source_target_pairs={{0,1},{1,0},{2,6},{3,7},{4,5},{5,4},{6,2},{7,3},{8,9},{9,8},{10,14... | collective-permute-start | bytes 1769480 | tf_op jit(solution)/shard_map/ppermute | solution.py:361
  57.0 12.7 %copy-start.41 = (bf16[192,1536]{1,0:T(8,128)(2,1)}, bf16[192,1536]{1,0:T(8,128)(2,1)S(1)}, u32[]{:S(2)}) copy-start(bf16[192,1536]{1,0:T(8,128)(2,1)S(1)} %collective-permute-done.5.refs_3_) | copy-start | bytes 1769476
  58.2 12.5 %copy-start.54 = (f32[768]{0:T(1024)S(1)}, f32[768]{0:T(1024)}, u32[]{:S(2)}) copy-start(f32[768]{0:T(1024)} %param.19) | copy-start | bytes 9220
  58.2 12.5 %copy-start.56 = (f32[768]{0:T(1024)S(1)}, f32[768]{0:T(1024)}, u32[]{:S(2)}) copy-start(f32[768]{0:T(1024)} %param.20) | copy-start | bytes 9220
  58.2 32.2 %collective-permute-start.6 = (bf16[384,1536]{1,0:T(8,128)(2,1)}, bf16[384,1536]{1,0:T(8,128)(2,1)}, u32[]{:S(2)}, u32[]{:S(2)}) collective-permute-start(bf16[384,1536]{1,0:T(8,128)(2,1)} %pad_maximum_fusion), channel_id=1, source_target_pairs={{0,4},{1,5},{2,3},{3,2},{4,0},{5,1},{6,7},{7,6},{8,12},{9,13},{10,... | collective-permute-start | bytes 3538952 | tf_op jit(solution)/shard_map/ppermute | solution.py:361
  69.7 19.3 %copy-start.60 = (f32[2,768]{1,0:T(2,128)S(1)}, f32[2,768]{1,0:T(2,128)}, u32[]{:S(2)}) copy-start(f32[2,768]{1,0:T(2,128)} %param.22) | copy-start | bytes 18436
  69.7 19.5 %copy-start.61 = (s32[16]{0:T(128)S(1)}, s32[16]{0:T(128)}, u32[]{:S(2)}) copy-start(s32[16]{0:T(128)} %constant.47.clone) | copy-start | bytes 196
  69.7 19.4 %copy-start.62 = (s32[16]{0:T(128)S(1)}, s32[16]{0:T(128)}, u32[]{:S(2)}) copy-start(s32[16]{0:T(128)} %constant.48.clone) | copy-start | bytes 196
  70.7 12.6 %copy-start.50 = (f32[768]{0:T(1024)}, f32[768]{0:T(1024)S(1)}, u32[]{:S(2)}) copy-start(f32[768]{0:T(1024)S(1)} %add_rsqrt_fusion.1) | copy-start | bytes 9220
  71.2 22.5 %copy-start.8 = (bf16[768,768]{1,0:T(8,128)(2,1)}, bf16[768,768]{1,0:T(8,128)(2,1)S(1)}, u32[]{:S(2)}) copy-start(bf16[768,768]{1,0:T(8,128)(2,1)S(1)} %fusion.9.refs_0_) | copy-start | bytes 3538948
  71.2 25.8 %collective-permute-start.7 = (bf16[768,768]{1,0:T(8,128)(2,1)S(1)}, bf16[768,768]{1,0:T(8,128)(2,1)}, u32[]{:S(2)}, u32[]{:S(2)}) collective-permute-start(bf16[768,768]{1,0:T(8,128)(2,1)S(1)} %fusion.9.refs_0_), channel_id=1, source_target_pairs={{0,2},{2,0},{1,3},{3,1},{4,6},{6,4},{5,7},{7,5},{8,10},{10,8},{9,1... | collective-permute-start | bytes 3538952 | tf_op jit(solution)/shard_map/ppermute | solution.py:393
  83.3 6.4 %collective-permute-start.1 = (s32[1]{0:T(128)}, s32[1]{0:T(128)}, u32[]{:S(2)}, u32[]{:S(2)}) collective-permute-start(s32[1]{0:T(128)} %param.18), channel_id=1, source_target_pairs={{0,0},{1,2},{2,1},{3,3},{4,4},{5,6},{6,5},{7,7},{8,8},{9,10},{10,9... | collective-permute-start | bytes 20 | tf_op jit(solution)/shard_map/ppermute | solution.py:384
  85.2 54.9 %collective-permute-start.9 = (bf16[768,768]{1,0:T(8,128)(2,1)}, bf16[768,768]{1,0:T(8,128)(2,1)}, u32[]{:S(2)}, u32[]{:S(2)}) collective-permute-start(bf16[768,768]{1,0:T(8,128)(2,1)} %param.31), channel_id=1, source_target_pairs={{1,2},{2,1},{5,6},{6,5},{9,10},{10,9},{13,14},{14,13},{17,18},{18,... | collective-permute-start | bytes 3538952 | tf_op jit(solution)/shard_map/ppermute | solution.py:388
  118.4 25.1 %copy-start.59 = (f32[768]{0:T(1024)S(1)}, f32[768]{0:T(1024)}, u32[]{:S(2)}) copy-start(f32[768]{0:T(1024)} %param.24) | copy-start | bytes 9220
  118.4 25.1 %collective-permute-start.8 = (bf16[768,768]{1,0:T(8,128)(2,1)}, bf16[768,768]{1,0:T(8,128)(2,1)}, u32[]{:S(2)}, u32[]{:S(2)}) collective-permute-start(bf16[768,768]{1,0:T(8,128)(2,1)} %convolution_convert_fusion.1), channel_id=1, source_target_pairs={{0,2},{2,0},{1,3},{3,1},{4,6},{6,4},{5,7},{7,5},{8,10},{10,8},{9,1... | collective-permute-start | bytes 3538952 | tf_op jit(solution)/shard_map/ppermute | solution.py:393
  143.5 6.0 %collective-permute-start.12 = (bf16[768,768]{1,0:T(8,128)(2,1)}, bf16[768,768]{1,0:T(8,128)(2,1)}, u32[]{:S(2)}, u32[]{:S(2)}) collective-permute-start(bf16[768,768]{1,0:T(8,128)(2,1)} %get-tuple-element.80.grad.refs_1_), channel_id=1, source_target_pairs={{0,2},{2,0},{1,3},{3,1},{4,6},{6,4},{5,7},{7,5},{8,10},{10,8},{9,1... | collective-permute-start | bytes 3538952 | tf_op jit(solution)/shard_map/ppermute | solution.py:393
  148.3 3.3 collective-permute-start.11
  169.5 15.5 %collective-permute-start.15 = (bf16[768,768]{1,0:T(8,128)(2,1)}, bf16[768,768]{1,0:T(8,128)(2,1)}, u32[]{:S(2)}, u32[]{:S(2)}) collective-permute-start(bf16[768,768]{1,0:T(8,128)(2,1)} %get-tuple-element.46), channel_id=1, source_target_pairs={{0,2},{2,0},{1,3},{3,1},{4,6},{6,4},{5,7},{7,5},{8,10},{10,8},{9,1... | collective-permute-start | bytes 3538952 | tf_op jit(solution)/shard_map/ppermute | solution.py:393
  169.9 19.6 %collective-permute-start.13 = (bf16[768,768]{1,0:T(8,128)(2,1)}, bf16[768,768]{1,0:T(8,128)(2,1)}, u32[]{:S(2)}, u32[]{:S(2)}) collective-permute-start(bf16[768,768]{1,0:T(8,128)(2,1)} %get-tuple-element.44), channel_id=1, source_target_pairs={{0,2},{2,0},{1,3},{3,1},{4,6},{6,4},{5,7},{7,5},{8,10},{10,8},{9,1... | collective-permute-start | bytes 3538952 | tf_op jit(solution)/shard_map/ppermute | solution.py:393
  173.7 11.4 %copy-start.23 = (f32[768,768]{1,0:T(8,128)S(1)}, f32[768,768]{1,0:T(8,128)}, u32[]{:S(2)}) copy-start(f32[768,768]{1,0:T(8,128)} %copy-done.22) | copy-start | bytes 7077892
  173.7 11.4 %copy-start.47 = (f32[768]{0:T(1024)S(1)}, f32[768]{0:T(1024)}, u32[]{:S(2)}) copy-start(f32[768]{0:T(1024)} %copy-done.46) | copy-start | bytes 9220
  173.7 11.4 %copy-start.49 = (f32[768]{0:T(1024)S(1)}, f32[768]{0:T(1024)}, u32[]{:S(2)}) copy-start(f32[768]{0:T(1024)} %param.25) | copy-start | bytes 9220
  189.5 5.7 %copy-start.34 = (bf16[768,1536]{1,0:T(8,128)(2,1)S(1)}, bf16[768,1536]{1,0:T(8,128)(2,1)}, u32[]{:S(2)}) copy-start(bf16[768,1536]{1,0:T(8,128)(2,1)} %place_blocks.1) | copy-start | bytes 7077892
  189.5 9.8 %copy-start.18 = (bf16[768,384]{1,0:T(8,128)(2,1)S(1)}, bf16[768,384]{1,0:T(8,128)(2,1)}, u32[]{:S(2)}) copy-start(bf16[768,384]{1,0:T(8,128)(2,1)} %copy-done.17) | copy-start | bytes 1769476
  194.8 4.6 copy-start.13
  194.8 4.6 copy-start.16
  194.8 4.6 copy-start.19
  194.8 2.9 collective-permute-start.16
  214.1 46.1 %collective-permute-start.17 = (bf16[384,3456]{1,0:T(8,128)(2,1)}, bf16[384,3456]{1,0:T(8,128)(2,1)}, u32[]{:S(2)}, u32[]{:S(2)}) collective-permute-start(bf16[384,3456]{1,0:T(8,128)(2,1)} %slice.94), channel_id=1, source_target_pairs={{0,4},{1,5},{2,3},{3,2},{4,0},{5,1},{6,7},{7,6},{8,12},{9,13},{10,... | collective-permute-start | bytes 7962632 | tf_op jit(solution)/shard_map/ppermute | solution.py:361
  217.2 144.7 %collective-permute-start.14 = (bf16[768,768]{1,0:T(8,128)(2,1)}, bf16[768,768]{1,0:T(8,128)(2,1)}, u32[]{:S(2)}, u32[]{:S(2)}) collective-permute-start(bf16[768,768]{1,0:T(8,128)(2,1)} %get-tuple-element.83), channel_id=1, source_target_pairs={{1,2},{2,1},{5,6},{6,5},{9,10},{10,9},{13,14},{14,13},{17,18},{18,... | collective-permute-start | bytes 3538952 | tf_op jit(solution)/shard_map/ppermute | solution.py:388
  266.1 112.6 %collective-permute-start.18 = (bf16[192,3456]{1,0:T(8,128)(2,1)}, bf16[192,3456]{1,0:T(8,128)(2,1)}, u32[]{:S(2)}, u32[]{:S(2)}) collective-permute-start(bf16[192,3456]{1,0:T(8,128)(2,1)} %slice.96), channel_id=1, source_target_pairs={{0,1},{1,0},{2,6},{3,7},{4,5},{5,4},{6,2},{7,3},{8,9},{9,8},{10,14... | collective-permute-start | bytes 3981320 | tf_op jit(solution)/shard_map/ppermute | solution.py:361
  365.4 13.2 %copy-start.28 = (bf16[384,3456]{1,0:T(8,128)(2,1)S(1)}, bf16[384,3456]{1,0:T(8,128)(2,1)}, u32[]{:S(2)}) copy-start(bf16[384,3456]{1,0:T(8,128)(2,1)} %copy-done.27) | copy-start | bytes 7962628
  381.7 27.7 %collective-permute-start.26 = (bf16[96,3456]{1,0:T(8,128)(2,1)}, bf16[96,3456]{1,0:T(8,128)(2,1)}, u32[]{:S(2)}, u32[]{:S(2)}) collective-permute-start(bf16[96,3456]{1,0:T(8,128)(2,1)} %slice.110), channel_id=1, source_target_pairs={{0,8},{1,9},{2,10},{3,11},{4,12},{5,13},{6,14},{7,15},{8,0},{9,1},... | collective-permute-start | bytes 1990664 | tf_op jit(solution)/shard_map/ppermute | solution.py:361
  395.3 6.4 %copy-start.3 = (bf16[768,1152]{1,0:T(8,128)(2,1)}, bf16[768,1152]{1,0:T(8,128)(2,1)S(1)}, u32[]{:S(2)}) copy-start(bf16[768,1152]{1,0:T(8,128)(2,1)S(1)} %constant_dynamic-update-slice_fusion.3.refs_3_) | copy-start | bytes 5308420
  402.7 12.5 %collective-permute-start.21 = (bf16[384,1152]{1,0:T(8,128)(2,1)}, bf16[384,1152]{1,0:T(8,128)(2,1)}, u32[]{:S(2)}, u32[]{:S(2)}) collective-permute-start(bf16[384,1152]{1,0:T(8,128)(2,1)} %slice.121), channel_id=1, source_target_pairs={{0,4},{1,5},{2,3},{3,2},{4,0},{5,1},{6,7},{7,6},{8,12},{9,13},{10,... | collective-permute-start | bytes 2654216 | tf_op jit(solution)/shard_map/ppermute | solution.py:361
  403.3 6.1 %copy-start.31 = (bf16[192,3456]{1,0:T(8,128)(2,1)S(1)}, bf16[192,3456]{1,0:T(8,128)(2,1)}, u32[]{:S(2)}) copy-start(bf16[192,3456]{1,0:T(8,128)(2,1)} %copy-done.30) | copy-start | bytes 3981316
  407.2 25.0 %collective-permute-start.19 = (bf16[768,768]{1,0:T(8,128)(2,1)S(1)}, bf16[768,768]{1,0:T(8,128)(2,1)S(1)}, u32[]{:S(2)}, u32[]{:S(2)}) collective-permute-start(bf16[768,768]{1,0:T(8,128)(2,1)S(1)} %convolution_convert_fusion), channel_id=1, source_target_pairs={{0,2},{2,0},{1,3},{3,1},{4,6},{6,4},{5,7},{7,5},{8,10},{10,8},{9,1... | collective-permute-start | bytes 3538952 | tf_op jit(solution)/shard_map/ppermute | solution.py:393
  409.4 22.8 %copy-start.35 = (bf16[768,1536]{1,0:T(8,128)(2,1)S(1)}, bf16[768,1536]{1,0:T(8,128)(2,1)}, u32[]{:S(2)}) copy-start(bf16[768,1536]{1,0:T(8,128)(2,1)} %place_blocks.1) | copy-start | bytes 7077892
  410.8 21.3 %copy-start.5 = (bf16[768,1152]{1,0:T(8,128)(2,1)S(1)}, bf16[768,1152]{1,0:T(8,128)(2,1)}, u32[]{:S(2)}) copy-start(bf16[768,1152]{1,0:T(8,128)(2,1)} %copy-done.4) | copy-start | bytes 5308420
  410.9 21.3 %copy-start.26 = (bf16[768,768]{1,0:T(8,128)(2,1)S(1)}, bf16[768,768]{1,0:T(8,128)(2,1)}, u32[]{:S(2)}) copy-start(bf16[768,768]{1,0:T(8,128)(2,1)} %copy-done.24) | copy-start | bytes 3538948
  410.9 21.3 %copy-start.45 = (f32[768]{0:T(1024)S(1)}, f32[768]{0:T(1024)}, u32[]{:S(2)}) copy-start(f32[768]{0:T(1024)} %copy-done.44) | copy-start | bytes 9220
  410.9 21.3 %copy-start.51 = (f32[768]{0:T(1024)S(1)}, f32[768]{0:T(1024)}, u32[]{:S(2)}) copy-start(f32[768]{0:T(1024)} %copy-done.50) | copy-start | bytes 9220
  410.9 21.3 %copy-start.55 = (f32[768]{0:T(1024)S(1)}, f32[768]{0:T(1024)}, u32[]{:S(2)}) copy-start(f32[768]{0:T(1024)} %param.19) | copy-start | bytes 9220
  410.9 17.5 %collective-permute-start.27 = (bf16[48,3456]{1,0:T(8,128)(2,1)S(1)}, bf16[48,3456]{1,0:T(8,128)(2,1)S(1)}, u32[]{:S(2)}, u32[]{:S(2)}) collective-permute-start(bf16[48,3456]{1,0:T(8,128)(2,1)S(1)} %slice.129), channel_id=1, source_target_pairs={{0,16},{1,17},{2,18},{3,19},{4,20},{5,21},{6,22},{7,23},{8,24},{9,... | collective-permute-start | bytes 995336 | tf_op jit(solution)/shard_map/ppermute | solution.py:361
  416.5 15.6 %copy-start.36 = (bf16[384,1152]{1,0:T(8,128)(2,1)}, bf16[384,1152]{1,0:T(8,128)(2,1)S(1)}, u32[]{:S(2)}) copy-start(bf16[384,1152]{1,0:T(8,128)(2,1)S(1)} %add_convert_fusion.4) | copy-start | bytes 2654212
  417.4 104.1 %collective-permute-start.22 = (bf16[192,1152]{1,0:T(8,128)(2,1)}, bf16[192,1152]{1,0:T(8,128)(2,1)}, u32[]{:S(2)}, u32[]{:S(2)}) collective-permute-start(bf16[192,1152]{1,0:T(8,128)(2,1)} %slice.123), channel_id=1, source_target_pairs={{0,1},{1,0},{2,6},{3,7},{4,5},{5,4},{6,2},{7,3},{8,9},{9,8},{10,14... | collective-permute-start | bytes 1327112 | tf_op jit(solution)/shard_map/ppermute | solution.py:361
  429.2 7.8 %copy-start.52 = (f32[1536]{0:T(1024)S(1)}, f32[1536]{0:T(1024)}, u32[]{:S(2)}) copy-start(f32[1536]{0:T(1024)} %reshape.117) | copy-start | bytes 18436
  429.2 100.4 %collective-permute-start.28 = (bf16[48,3456]{1,0:T(8,128)(2,1)}, bf16[48,3456]{1,0:T(8,128)(2,1)}, u32[]{:S(2)}, u32[]{:S(2)}) collective-permute-start(bf16[48,3456]{1,0:T(8,128)(2,1)} %add_convert_fusion.7), channel_id=1, source_target_pairs={{0,0},{1,2},{2,1},{3,3},{4,4},{5,6},{6,5},{7,7},{8,8},{9,10},{10,9... | collective-permute-start | bytes 995336 | tf_op jit(solution)/shard_map/ppermute | solution.py:384
  432.2 81.0 %copy-start.29 = (f32[768,768]{1,0:T(8,128)S(1)}, f32[768,768]{1,0:T(8,128)}, u32[]{:S(2)}) copy-start(f32[768,768]{1,0:T(8,128)} %get-tuple-element.78) | copy-start | bytes 7077892
  513.2 8.4 %copy-start.37 = (bf16[384,1152]{1,0:T(8,128)(2,1)S(1)}, bf16[384,1152]{1,0:T(8,128)(2,1)}, u32[]{:S(2)}) copy-start(bf16[384,1152]{1,0:T(8,128)(2,1)} %copy-done.36) | copy-start | bytes 2654212
  516.4 28.0 %collective-permute-start.20 = (bf16[768,768]{1,0:T(8,128)(2,1)}, bf16[768,768]{1,0:T(8,128)(2,1)S(1)}, u32[]{:S(2)}, u32[]{:S(2)}) collective-permute-start(bf16[768,768]{1,0:T(8,128)(2,1)} %fusion.14), channel_id=1, source_target_pairs={{1,2},{2,1},{5,6},{6,5},{9,10},{10,9},{13,14},{14,13},{17,18},{18,... | collective-permute-start | bytes 3538952 | tf_op jit(solution)/shard_map/ppermute | solution.py:388
  522.7 6.7 %collective-permute-start.23 = (bf16[96,1152]{1,0:T(8,128)(2,1)S(1)}, bf16[96,1152]{1,0:T(8,128)(2,1)S(1)}, u32[]{:S(2)}, u32[]{:S(2)}) collective-permute-start(bf16[96,1152]{1,0:T(8,128)(2,1)S(1)} %slice.125), channel_id=1, source_target_pairs={{0,8},{1,9},{2,10},{3,11},{4,12},{5,13},{6,14},{7,15},{8,0},{9,1},... | collective-permute-start | bytes 663560 | tf_op jit(solution)/shard_map/ppermute | solution.py:361
  529.5 7.8 %collective-permute-start.24 = (bf16[48,1152]{1,0:T(8,128)(2,1)S(1)}, bf16[48,1152]{1,0:T(8,128)(2,1)S(1)}, u32[]{:S(2)}, u32[]{:S(2)}) collective-permute-start(bf16[48,1152]{1,0:T(8,128)(2,1)S(1)} %slice.127), channel_id=1, source_target_pairs={{0,16},{1,17},{2,18},{3,19},{4,20},{5,21},{6,22},{7,23},{8,24},{9,... | collective-permute-start | bytes 331784 | tf_op jit(solution)/shard_map/ppermute | solution.py:361
  537.3 6.1 %collective-permute-start.25 = (bf16[48,1152]{1,0:T(8,128)(2,1)S(1)}, bf16[48,1152]{1,0:T(8,128)(2,1)S(1)}, u32[]{:S(2)}, u32[]{:S(2)}) collective-permute-start(bf16[48,1152]{1,0:T(8,128)(2,1)S(1)} %add_convert_fusion.9), channel_id=1, source_target_pairs={{0,0},{1,2},{2,1},{3,3},{4,4},{5,6},{6,5},{7,7},{8,8},{9,10},{10,9... | collective-permute-start | bytes 331784 | tf_op jit(solution)/shard_map/ppermute | solution.py:384
  (29 other events, 57.9 us)
Sparse Core Ops, SparseCore 0:
  18.1 99.7 all-gather.3
